TPU v7x, 32 devices: a whole 2x2x4 slice. The times are simulated.
32 devices in a mesh: dp: 8 (over z, x), expert: 4 (over y, core).
Axes of the slice: x: 2, y: 2, z: 4, core: 2. Of those that a mesh axis runs over, the one named last changes fastest.
Arguments:
- tokens: bfloat16 [2, 16384, 768], P(None, ('dp', 'expert')), may hold values from -6 to 6
- routes: int32 [2, 16384, 2], P(None, ('dp', 'expert')), may hold values from 0 to 5, all different within a row
- lengths: int32 [2, 32, 4], P(None, ('dp', 'expert')), may hold values from 1 to 320, 512 in all within a row
- key_mask: int32 [2, 16384], P(None, ('dp', 'expert')), may hold values 0 or 1
- gain_one: float32 [768], replicated, may hold values from 0.5 to 1.5
- bias_one: float32 [768], replicated, may hold values from -1 to 1
- w_query: bfloat16 [768, 768], replicated, may hold values from -0.21875 to 0.21875
- w_key: bfloat16 [768, 768], replicated, may hold values from -0.21875 to 0.21875
- w_value: bfloat16 [768, 768], replicated, may hold values from -0.21875 to 0.21875
- w_output: bfloat16 [768, 768], replicated, may hold values from -0.625 to 0.625
- gain_two: float32 [768], replicated, may hold values from 0.5 to 1.5
- bias_two: float32 [768], replicated, may hold values from -1 to 1
- w_router: bfloat16 [768, 6], replicated, may hold values from -0.15625 to 0.15625
- frozen_in: bfloat16 [2, 768, 3072], replicated, may hold values from -0.21875 to 0.21875
- frozen_out: bfloat16 [2, 3072, 768], replicated, may hold values from -0.109375 to 0.109375
- new_in: float32 [4, 768, 3072], P('expert', None, 'dp'), may hold values from -0.21875 to 0.21875
- new_out: float32 [4, 3072, 768], P('expert', 'dp'), may hold values from -0.109375 to 0.109375
- cotangent: bfloat16 [2, 16384, 768], P(None, ('dp', 'expert')), may hold values from -6 to 6
Outputs:
- mixed: bfloat16 [2, 16384, 768], P(None, ('dp', 'expert'))
- input_grad: bfloat16 [2, 16384, 768], P(None, ('dp', 'expert'))
- gain_one_grad: float32 [768], P(('dp', 'expert'))
- bias_one_grad: float32 [768], P(('dp', 'expert'))
- query_grad: float32 [768, 768], P(('dp', 'expert'))
- key_grad: float32 [768, 768], P(('dp', 'expert'))
- value_grad: float32 [768, 768], P(('dp', 'expert'))
- output_grad: float32 [768, 768], P(('dp', 'expert'))
- gain_two_grad: float32 [768], P(('dp', 'expert'))
- bias_two_grad: float32 [768], P(('dp', 'expert'))
- router_grad: float32 [768, 6], P(('dp', 'expert'))
- new_in_grad: float32 [4, 768, 3072], P('expert', None, 'dp')
- new_out_grad: float32 [4, 3072, 768], P('expert', 'dp')
Inputs may be any that keep to these rules, and one draw needn't show every extreme that they name: `routes`: the two picks of a row differ and every expert is named by some row; a block may name an expert more than 208 times. Each block's 4 lengths sum to 512, the largest exactly 320.
All inputs are finite; a program needn't handle non-finite values. No bound on the sum of `key_mask` on one device may be relied on, other than what follows from the above.
Results may differ from a plain program's by a relative error of at most 0.014.
Values may be sent and summed in bfloat16 or wider, within the bound.
A program may use at most 320 MiB of HBM per device.

v0:
```python
import jax
import jax.numpy as jnp
from jax import lax
from jax.sharding import PartitionSpec as P

HEAD = 64


epsilon = 1e-05


def norm_forward(values, gain, shift):
    center = values - jnp.mean(values, -1, keepdims=True)
    inverse = lax.rsqrt(jnp.mean(center * center, -1, keepdims=True) + epsilon)
    unit_rows = center * inverse
    return (unit_rows * gain + shift, unit_rows, inverse)


def norm_backward(grad_norm, unit_rows, inverse, gain):
    scaled = grad_norm * gain
    grad_in = inverse * (
        scaled
        - jnp.mean(scaled, -1, keepdims=True)
        - unit_rows * jnp.mean(scaled * unit_rows, -1, keepdims=True)
    )
    return (grad_in, jnp.sum(grad_norm * unit_rows, 0), jnp.sum(grad_norm, 0))


def visible_mask(block_lengths, block_mask, tok_rows):
    places = jnp.arange(tok_rows, dtype=jnp.int32)
    ends = jnp.cumsum(block_lengths)
    doc_ids = jnp.sum((places[:, None] >= ends[None, :]).astype(jnp.int32), 1)
    same_doc = doc_ids[:, None] == doc_ids[None, :]
    causal = places[None, :] <= places[:, None]
    keep_key = (block_mask[None, :] == 1) | (places[None, :] == places[:, None])
    return same_doc & causal & keep_key


def slot_tables(route_rows, experts_all, capacity):
    expert_ids = jnp.arange(experts_all, dtype=jnp.int32)
    pick_hot = [
        (route_rows[:, pick_no][:, None] == expert_ids[None, :]).astype(jnp.int32)
        for pick_no in range(2)
    ]
    chosen_hot = pick_hot[0] + pick_hot[1]
    earlier = jnp.cumsum(chosen_hot, 0) - chosen_hot
    slot_ids = jnp.arange(capacity, dtype=jnp.int32)
    slot_match = earlier.T[:, None, :] == slot_ids[None, :, None]
    hots = [
        jnp.where(slot_match & (pick_hot[pick_no].T[:, None, :] == 1), 1.0, 0.0).astype(
            jnp.bfloat16
        )
        for pick_no in range(2)
    ]
    return ([table.astype(jnp.float32) for table in pick_hot], hots)


def tree_add(first, second):
    if first is None:
        return second
    return jax.tree.map(jnp.add, first, second)


def per_device(
    tokens,
    routes,
    lengths,
    key_mask,
    gain_one,
    bias_one,
    w_query,
    w_key,
    w_value,
    w_output,
    gain_two,
    bias_two,
    w_router,
    frozen_in,
    frozen_out,
    new_in,
    new_out,
    cotangent,
):
    half = jnp.bfloat16
    single = jnp.float32
    micro_count, tok_rows, width = tokens.shape
    owners = lax.axis_size("expert")
    per_owner = new_in.shape[0]
    frozen_count = frozen_in.shape[0]
    experts_all = frozen_count + owners * per_owner
    capacity = 10 * tok_rows // (4 * experts_all) // 8 * 8
    heads_count = width // HEAD
    scale_factor = HEAD ** (-0.5)
    in_full, out_full = (
        lax.all_gather(new_in.astype(half), "dp", axis=2, tiled=True),
        lax.all_gather(new_out.astype(half), "dp", axis=1, tiled=True),
    )
    shared_total = None
    expert_total = None
    mixed_list = []
    grad_list = []
    for micro_no in range(micro_count):
        values = tokens[micro_no].astype(single)
        visible = visible_mask(lengths[micro_no, 0], key_mask[micro_no], tok_rows)
        normed, unit_one, inv_one = norm_forward(values, gain_one, bias_one)
        normed_low = normed.astype(half)
        queries = (
            jnp.dot(normed_low, w_query, preferred_element_type=single)
            .astype(half)
            .reshape(tok_rows, heads_count, HEAD)
        )
        key_rows = (
            jnp.dot(normed_low, w_key, preferred_element_type=single)
            .astype(half)
            .reshape(tok_rows, heads_count, HEAD)
        )
        value_rows = (
            jnp.dot(normed_low, w_value, preferred_element_type=single)
            .astype(half)
            .reshape(tok_rows, heads_count, HEAD)
        )
        scores = (
            jnp.einsum("thd,shd->hts", queries, key_rows, preferred_element_type=single)
            * scale_factor
        )
        scores = jnp.where(visible[None], scores, -1000000000.0)
        top_score = jnp.max(scores, -1, keepdims=True)
        expo = jnp.exp(scores - top_score)
        total_exp = jnp.sum(expo, -1, keepdims=True)
        log_total = top_score + jnp.log(total_exp)
        probs_low = (expo / total_exp).astype(half)
        attended = (
            jnp.einsum("hts,shd->thd", probs_low, value_rows, preferred_element_type=single)
            .astype(half)
            .reshape(tok_rows, width)
        )
        middle = values + jnp.dot(attended, w_output, preferred_element_type=single)
        second, unit_two, inv_two = norm_forward(middle, gain_two, bias_two)
        second_low = second.astype(half)
        logits = jnp.dot(second_low, w_router, preferred_element_type=single)
        router_probs = jax.nn.softmax(logits, -1)
        pick_hot, hots = slot_tables(routes[micro_no], experts_all, capacity)
        chosen = [jnp.sum(router_probs * pick_hot[pick_no], -1) for pick_no in range(2)]
        chosen_total = chosen[0] + chosen[1]
        gates = [chosen[pick_no] / chosen_total for pick_no in range(2)]
        place = hots[0] + hots[1]
        buffers = jnp.einsum(
            "ect,td->ecd", place, second_low, preferred_element_type=single
        ).astype(half)
        frozen_pre = jnp.einsum(
            "ecd,edf->ecf", buffers[:frozen_count], frozen_in, preferred_element_type=single
        )
        frozen_hidden = jax.nn.gelu(frozen_pre).astype(half)
        frozen_result = jnp.einsum(
            "ecf,efd->ecd", frozen_hidden, frozen_out, preferred_element_type=single
        ).astype(half)
        outgoing = buffers[frozen_count:].reshape(owners, per_owner, capacity, width)
        arrived = lax.all_to_all(outgoing, "expert", split_axis=0, concat_axis=0, tiled=True)
        pre_act = jnp.einsum("spnd,pdf->spnf", arrived, in_full, preferred_element_type=single)
        hidden = jax.nn.gelu(pre_act).astype(half)
        produced = jnp.einsum(
            "spnf,pfd->spnd", hidden, out_full, preferred_element_type=single
        ).astype(half)
        returned = lax.all_to_all(produced, "expert", split_axis=0, concat_axis=0, tiled=True)
        results = jnp.concatenate(
            [frozen_result, returned.reshape(owners * per_owner, capacity, width)], 0
        )
        picked = [
            jnp.einsum("ect,ecd->td", hots[pick_no], results, preferred_element_type=single)
            for pick_no in range(2)
        ]
        output_rows = middle + gates[0][:, None] * picked[0] + gates[1][:, None] * picked[1]
        mixed_list.append(output_rows.astype(half))
        grad_out = cotangent[micro_no].astype(single)
        grad_gates = [jnp.sum(grad_out * picked[pick_no], -1) for pick_no in range(2)]
        grad_results = jnp.einsum(
            "ect,td->ecd",
            hots[0],
            (gates[0][:, None] * grad_out).astype(half),
            preferred_element_type=single,
        )
        grad_results = grad_results + jnp.einsum(
            "ect,td->ecd",
            hots[1],
            (gates[1][:, None] * grad_out).astype(half),
            preferred_element_type=single,
        )
        grad_results = grad_results.astype(half)
        grad_frozen_hidden = jnp.einsum(
            "ecd,efd->ecf", grad_results[:frozen_count], frozen_out, preferred_element_type=single
        )
        frozen_value, frozen_pull = jax.vjp(jax.nn.gelu, frozen_pre)
        grad_frozen_pre = frozen_pull(grad_frozen_hidden)[0].astype(half)
        grad_frozen_buf = jnp.einsum(
            "ecf,edf->ecd", grad_frozen_pre, frozen_in, preferred_element_type=single
        ).astype(half)
        grad_sent = grad_results[frozen_count:].reshape(owners, per_owner, capacity, width)
        grad_arrived = lax.all_to_all(grad_sent, "expert", split_axis=0, concat_axis=0, tiled=True)
        grad_hidden = jnp.einsum(
            "spnd,pfd->spnf", grad_arrived, out_full, preferred_element_type=single
        )
        hidden_value, hidden_pull = jax.vjp(jax.nn.gelu, pre_act)
        grad_pre = hidden_pull(grad_hidden)[0].astype(half)
        grad_buf_new = jnp.einsum(
            "spnf,pdf->spnd", grad_pre, in_full, preferred_element_type=single
        ).astype(half)
        grad_buf_back = lax.all_to_all(
            grad_buf_new, "expert", split_axis=0, concat_axis=0, tiled=True
        )
        hidden_again = hidden_value.astype(half)
        step_in = jnp.einsum("spnd,spnf->pdf", arrived, grad_pre, preferred_element_type=single)
        step_out = jnp.einsum(
            "spnf,spnd->pfd", hidden_again, grad_arrived, preferred_element_type=single
        )
        grad_buffers = jnp.concatenate(
            [grad_frozen_buf, grad_buf_back.reshape(owners * per_owner, capacity, width)], 0
        )
        grad_second = jnp.einsum("ect,ecd->td", place, grad_buffers, preferred_element_type=single)
        weighted = grad_gates[0] * gates[0] + grad_gates[1] * gates[1]
        grad_router_probs = ((grad_gates[0] - weighted) / chosen_total)[:, None] * pick_hot[0]
        grad_router_probs = (
            grad_router_probs + ((grad_gates[1] - weighted) / chosen_total)[:, None] * pick_hot[1]
        )
        grad_logits = router_probs * (
            grad_router_probs - jnp.sum(grad_router_probs * router_probs, -1, keepdims=True)
        )
        logits_low = grad_logits.astype(half)
        step_router = jnp.dot(second_low.T, logits_low, preferred_element_type=single)
        grad_second = grad_second + jnp.dot(logits_low, w_router.T, preferred_element_type=single)
        grad_middle_part, step_gain_two, step_bias_two = norm_backward(
            grad_second, unit_two, inv_two, gain_two
        )
        grad_middle = grad_out + grad_middle_part
        branch_low = grad_middle.astype(half)
        step_output = jnp.dot(attended.T, branch_low, preferred_element_type=single)
        grad_attended = (
            jnp.dot(branch_low, w_output.T, preferred_element_type=single)
            .astype(half)
            .reshape(tok_rows, heads_count, HEAD)
        )
        again = (
            jnp.einsum("thd,shd->hts", queries, key_rows, preferred_element_type=single)
            * scale_factor
        )
        again = jnp.where(visible[None], again, -1000000000.0)
        probs_again = jnp.exp(again - log_total)
        grad_value_rows = (
            jnp.einsum(
                "hts,thd->shd",
                probs_again.astype(half),
                grad_attended,
                preferred_element_type=single,
            )
            .astype(half)
            .reshape(tok_rows, width)
        )
        grad_probs = jnp.einsum(
            "thd,shd->hts", grad_attended, value_rows, preferred_element_type=single
        )
        grad_scores = (
            probs_again * (grad_probs - jnp.sum(grad_probs * probs_again, -1, keepdims=True))
        ).astype(half)
        grad_queries = (
            (
                jnp.einsum("hts,shd->thd", grad_scores, key_rows, preferred_element_type=single)
                * scale_factor
            )
            .astype(half)
            .reshape(tok_rows, width)
        )
        grad_key_rows = (
            (
                jnp.einsum("hts,thd->shd", grad_scores, queries, preferred_element_type=single)
                * scale_factor
            )
            .astype(half)
            .reshape(tok_rows, width)
        )
        step_query = jnp.dot(normed_low.T, grad_queries, preferred_element_type=single)
        step_key = jnp.dot(normed_low.T, grad_key_rows, preferred_element_type=single)
        step_value = jnp.dot(normed_low.T, grad_value_rows, preferred_element_type=single)
        grad_normed = jnp.dot(grad_queries, w_query.T, preferred_element_type=single)
        grad_normed = grad_normed + jnp.dot(grad_key_rows, w_key.T, preferred_element_type=single)
        grad_normed = grad_normed + jnp.dot(
            grad_value_rows, w_value.T, preferred_element_type=single
        )
        grad_in_part, step_gain_one, step_bias_one = norm_backward(
            grad_normed, unit_one, inv_one, gain_one
        )
        grad_list.append((grad_middle + grad_in_part).astype(half))
        shared_done = (
            lax.psum_scatter(step_query, ("dp", "expert"), scatter_dimension=0, tiled=True),
            lax.psum_scatter(step_key, ("dp", "expert"), scatter_dimension=0, tiled=True),
            lax.psum_scatter(step_value, ("dp", "expert"), scatter_dimension=0, tiled=True),
            lax.psum_scatter(step_output, ("dp", "expert"), scatter_dimension=0, tiled=True),
            lax.psum_scatter(step_router, ("dp", "expert"), scatter_dimension=0, tiled=True),
            lax.psum_scatter(step_gain_one, ("dp", "expert"), scatter_dimension=0, tiled=True),
            lax.psum_scatter(step_bias_one, ("dp", "expert"), scatter_dimension=0, tiled=True),
            lax.psum_scatter(step_gain_two, ("dp", "expert"), scatter_dimension=0, tiled=True),
            lax.psum_scatter(step_bias_two, ("dp", "expert"), scatter_dimension=0, tiled=True),
        )
        expert_done = (
            lax.psum_scatter(
                step_in.astype(jnp.bfloat16), "dp", scatter_dimension=2, tiled=True
            ).astype(jnp.float32),
            lax.psum_scatter(
                step_out.astype(jnp.bfloat16), "dp", scatter_dimension=1, tiled=True
            ).astype(jnp.float32),
        )
        shared_total = tree_add(shared_total, shared_done)
        expert_total = tree_add(expert_total, expert_done)
    mixed = jnp.stack(mixed_list, 0)
    input_grad = jnp.stack(grad_list, 0)
    return (
        mixed,
        input_grad,
        shared_total[5],
        shared_total[6],
        shared_total[0],
        shared_total[1],
        shared_total[2],
        shared_total[3],
        shared_total[7],
        shared_total[8],
        shared_total[4],
        expert_total[0],
        expert_total[1],
    )


def solution(mesh):
    return jax.shard_map(
        per_device,
        mesh=mesh,
        in_specs=(
            P(None, ("dp", "expert"), None),
            P(None, ("dp", "expert"), None),
            P(None, ("dp", "expert"), None),
            P(None, ("dp", "expert")),
            P(),
            P(),
            P(),
            P(),
            P(),
            P(),
            P(),
            P(),
            P(),
            P(),
            P(),
            P("expert", None, "dp"),
            P("expert", "dp", None),
            P(None, ("dp", "expert"), None),
        ),
        out_specs=(
            P(None, ("dp", "expert"), None),
            P(None, ("dp", "expert"), None),
            P(("dp", "expert")),
            P(("dp", "expert")),
            P(("dp", "expert"), None),
            P(("dp", "expert"), None),
            P(("dp", "expert"), None),
            P(("dp", "expert"), None),
            P(("dp", "expert")),
            P(("dp", "expert")),
            P(("dp", "expert"), None),
            P("expert", None, "dp"),
            P("expert", "dp", None),
        ),
        check_vma=False,
    )
```

profile of v0, /device:TPU:0, one launch (start us, length us, event | category | flops | bytes accessed | tf_op | source)
XLA Modules:
  0.0 1122.2 jit_solution(9936325335057958752)
XLA Ops:
  93.1 8.5 fusion.436
  107.9 8.2 fusion.435
  126.9 10.7 fusion.68
  137.6 36.6 %all-gather.5.cloned.1.call-done = bf16[1,3072,768]{2,1,0:T(8,128)(2,1)} async-done(((bf16[1,384,768]{2,1,0:T(8,128)(2,1)}), bf16[1,3072,768]{2,1,0:T(8,128)(2,1)}) %all-gather.5.cloned.1.call-update) | async-done | bytes 4718608 | tf_op jit(solution)/shard_map/all_gather | solution.py:96
  174.1 12.3 %fusion.214 = bf16[4,1,208,768]{3,2,1,0:T(8,128)(2,1)} fusion(bf16[1,3072,768]{2,1,0:T(8,128)(2,1)} %all-gather.5.cloned.1.call-done, f32[4,208,3072]{2,1,0:T(8,128)} %fusion.68), kind=kOutput, calls=%fused_computation.260 | convolution fusion | flops 3949510656 | bytes 16220160 | tf_op jit(solution)/shard_map/spnf,pfd->spnd/dot_general | solution.py:161
  220.9 8.8 all-to-all-done.1
  241.9 19.6 %all_to_all.40 = bf16[4,1,208,768]{3,2,1,0:T(8,128)(2,1)S(1)} all-to-all(bf16[4,1,208,768]{3,2,1,0:T(8,128)(2,1)S(1)} %slice_bitcast_fusion), channel_id=1, replica_groups=mesh['dp'=8,'expert'=4] {'expert'}, dimensions={0} | all-to-all | bytes 2555904 | tf_op jit(solution)/shard_map/all_to_all | solution.py:198
  261.6 9.5 fusion.15
  273.3 8.1 fusion.75
  281.4 20.4 %copy.145 = bf16[1,768,3072]{1,0,2:T(2,128)(2,1)} copy(bf16[1,768,3072]{2,1,0:T(8,128)(2,1)} %fusion.75) | data formatting | bytes 9437184
  314.9 19.8 %all_to_all.41 = bf16[4,1,208,768]{3,2,1,0:T(8,128)(2,1)S(1)} all-to-all(bf16[4,1,208,768]{3,2,1,0:T(8,128)(2,1)S(1)} %slice_bitcast_fusion.1), channel_id=1, replica_groups=mesh['dp'=8,'expert'=4] {'expert'}, dimensions={0} | all-to-all | bytes 2555904 | tf_op jit(solution)/shard_map/all_to_all | solution.py:198
  334.7 12.2 %fusion.8 = bf16[4,1,208,3072]{3,2,0,1:T(8,128)(2,1)S(1)} fusion(f32[4,208,3072]{2,1,0:T(8,128)} %copy-done.123, bf16[1,3072,768]{2,1,0:T(8,128)(2,1)S(1)} %bitcast.666, bf16[4,1,208,768]{3,2,1,0:T(8,128)(2,1)S(1)} %all_to_all.41), kind=kOutput, calls=%fused_computation.24 | convolution fusion | flops 3976986624 | bytes 21331968 | tf_op jit(solution)/shard_map/spnd,pfd->spnf/dot_general | solution.py:199
  349.1 8.2 fusion.72
  357.3 20.5 %copy.143 = bf16[1,768,3072]{1,0,2:T(2,128)(2,1)} copy(bf16[1,768,3072]{2,1,0:T(8,128)(2,1)} %fusion.72) | data formatting | bytes 9437184
  384.9 11.5 %fusion.78 = bf16[1,3072,768]{2,1,0:T(8,128)(2,1)} fusion(f32[4,208,3072]{2,1,0:T(8,128)} %copy-done.123, bf16[4,1,208,768]{3,2,1,0:T(8,128)(2,1)} %copy-done.52), kind=kOutput, calls=%fused_computation.106 | convolution fusion | flops 3951230976 | bytes 16220160 | tf_op jit(solution)/shard_map/spnf,spnd->pfd/dot_general | solution.py:212
  400.1 9.5 fusion.438
  409.6 9.5 fusion.437
  419.2 12.6 %fusion.235 = bf16[2,208,768]{2,1,0:T(8,128)(2,1)} fusion(bf16[2,768,3072]{2,1,0:T(8,128)(2,1)} %param.31, f32[2,208,3072]{2,1,0:T(8,128)} %fusion.436, f32[2,208,3072]{2,1,0:T(8,128)} %fusion.438), kind=kOutput, calls=%fused_computation.279 | convolution fusion | flops 1988812800 | bytes 20299776 | tf_op jit(solution)/shard_map/ecf,edf->ecd/dot_general | solution.py:194
  431.8 13.0 %fusion.232 = bf16[2,208,768]{2,1,0:T(8,128)(2,1)} fusion(bf16[2,768,3072]{2,1,0:T(8,128)(2,1)} %param.31, f32[2,208,3072]{2,1,0:T(8,128)} %fusion.435, f32[2,208,3072]{2,1,0:T(8,128)} %fusion.437), kind=kOutput, calls=%fused_computation.278 | convolution fusion | flops 1988812800 | bytes 20299776 | tf_op jit(solution)/shard_map/ecf,edf->ecd/dot_general | solution.py:194
  444.7 11.5 %fusion.81 = bf16[1,3072,768]{2,1,0:T(8,128)(2,1)} fusion(f32[4,208,3072]{2,1,0:T(8,128)} %fusion.68, bf16[4,1,208,768]{3,2,1,0:T(8,128)(2,1)} %copy-done.50), kind=kOutput, calls=%fused_computation.107 | convolution fusion | flops 3951230976 | bytes 16220160 | tf_op jit(solution)/shard_map/spnf,spnd->pfd/dot_general | solution.py:212
  456.4 9.3 fusion.209
  469.7 9.1 fusion.204
  495.1 12.7 %all-to-all-done.7 = bf16[4,1,208,768]{3,2,1,0:T(8,128)(2,1)} async-done(((bf16[4,1,208,768]{3,2,1,0:T(8,128)(2,1)}), bf16[4,1,208,768]{3,2,1,0:T(8,128)(2,1)}, u32[]{:S(2)}, u32[]{:S(2)}) %all-to-all-start.7) | async-done | bytes 1277984 | tf_op jit(solution)/shard_map/all_to_all | solution.py:207
  528.1 8.4 fusion.224
  542.9 13.6 %multiply_reduce_fusion.1 = (f32[12,512]{1,0:T(8,128)S(1)}, f32[12,512,512]{1,2,0:T(8,128)}) fusion(f32[12,512]{1,0:T(8,128)S(1)} %copy-done.68, f32[12,512,512]{1,2,0:T(8,128)} %copy-done.2, pred[512,512]{0,1:T(8,128)(4,1)S(1)} %copy-done.31, bf16[512,12,64]{0,2,1:T(8,128)(2,1)} %bitcast.613, bf16[512,12,64]{0,2,1:T(8,128)(2,1)} %bitcast.609), kind=kOutput, calls=%fused_computation.8 | convolution fusion | flops 418375680 | bytes 27049984 | tf_op jit(solution)/shard_map/thd,shd->hts/dot_general | solution.py:257
  556.6 10.3 multiply_convert_fusion.1
  582.4 9.4 multiply_reduce_fusion
  635.3 39.4 %all-reduce.5 = (f32[768]{0:T(1024)}, f32[768]{0:T(1024)}, f32[768]{0:T(1024)}, f32[768]{0:T(1024)}, f32[768,6]{0,1:T(8,128)}) all-reduce(f32[768]{0:T(1024)} %add.399, f32[768]{0:T(1024)} %add.400, f32[768]{0:T(1024)} %add.405, f32[768]{0:T(1024)} %add.406, ...), channel_id=11, replica_groups=mesh['dp'=8,'expert'=4] {'dp','expert'}, use_global_device_ids=true, to_apply=%region_45.46.clone | all-reduce | flops 7680 | bytes 61440
  699.3 102.4 %reduce-scatter.24.cloned.1.call-done = f32[24,768]{1,0:T(8,128)} async-done(((f32[768,768]{1,0:T(8,128)}), f32[24,768]{1,0:T(8,128)}) %reduce-scatter.24.cloned.1.call-update) | async-done | bytes 73744 | tf_op jit(solution)/shard_map/reduce_scatter | solution.py:295
  801.7 104.8 %reduce-scatter.22.cloned.1.call-done = f32[24,768]{1,0:T(8,128)} async-done(((f32[768,768]{1,0:T(8,128)}), f32[24,768]{1,0:T(8,128)}) %reduce-scatter.22.cloned.1.call-update) | async-done | bytes 73744 | tf_op jit(solution)/shard_map/reduce_scatter | solution.py:294
  906.5 104.0 %reduce-scatter.20.cloned.1.call-done = f32[24,768]{1,0:T(8,128)} async-done(((f32[768,768]{1,0:T(8,128)}), f32[24,768]{1,0:T(8,128)}) %reduce-scatter.20.cloned.1.call-update) | async-done | bytes 73744 | tf_op jit(solution)/shard_map/reduce_scatter | solution.py:293
  1010.6 104.6 %reduce-scatter.18.cloned.1.call-done = f32[24,768]{1,0:T(8,128)} async-done(((f32[768,768]{1,0:T(8,128)}), f32[24,768]{1,0:T(8,128)}) %reduce-scatter.18.cloned.1.call-update) | async-done | bytes 73744 | tf_op jit(solution)/shard_map/reduce_scatter | solution.py:292
  (482 shorter events, 307.2 us)
Async XLA Ops:
  7.2 119.7 %all-gather.3.cloned.1.call-start = ((), (), s32[]{:S(2)}) async-start(), calls=%async_computation.16 | async-start | bytes 5308416 | tf_op jit(solution)/shard_map/all_gather | solution.py:95
  9.5 164.6 %all-gather.5.cloned.1.call-start = ((), (), s32[]{:S(2)}) async-start(), calls=%async_computation.17 | async-start | bytes 5308416 | tf_op jit(solution)/shard_map/all_gather | solution.py:96
  32.3 29.5 %copy-start.19 = (bf16[512,768]{0,1:T(8,128)(2,1)}, bf16[512,768]{0,1:T(8,128)(2,1)S(1)}, u32[]{:S(2)}) copy-start(bf16[512,768]{0,1:T(8,128)(2,1)S(1)} %copy.117) | copy-start | bytes 2359300
  60.7 14.8 %copy-start.80 = (f32[512]{0:T(512)}, f32[512]{0:T(512)S(1)}, u32[]{:S(2)}) copy-start(f32[512]{0:T(512)S(1)} %broadcast_multiply_fusion.10) | copy-start | bytes 6148
  77.1 161.9 %copy-start.97 = (s32[6,512]{1,0:T(8,128)}, s32[6,512]{1,0:T(8,128)S(1)}, u32[]{:S(2)}) copy-start(s32[6,512]{1,0:T(8,128)S(1)} %fusion.328) | copy-start | bytes 36868
  82.0 40.1 %all-to-all-start.2 = ((bf16[4,1,208,768]{3,2,1,0:T(8,128)(2,1)}), bf16[4,1,208,768]{3,2,1,0:T(8,128)(2,1)}, u32[]{:S(2)}, u32[]{:S(2)}) async-start(bf16[4,1,208,768]{3,2,1,0:T(8,128)(2,1)} %slice_bitcast_fusion.2), calls=%async_computation.2 | async-start | bytes 2555904 | tf_op jit(solution)/shard_map/all_to_all | solution.py:158
  122.1 64.3 %all-to-all-start = ((bf16[4,1,208,768]{3,2,1,0:T(8,128)(2,1)}), bf16[4,1,208,768]{3,2,1,0:T(8,128)(2,1)}, u32[]{:S(2)}, u32[]{:S(2)}) async-start(bf16[4,1,208,768]{3,2,1,0:T(8,128)(2,1)} %slice_bitcast_fusion.3), calls=%async_computation | async-start | bytes 2555904 | tf_op jit(solution)/shard_map/all_to_all | solution.py:158
  186.4 14.9 %slice-start.5 = ((s8[4718592]{0:T(1024)(128)(4,1)}), s8[524288]{0:T(1024)(128)(4,1)S(1)}, s32[]{:S(2)}) async-start(s8[4718592]{0:T(1024)(128)(4,1)} %bitcast.661), calls=%async_computation.31 | async-start | bytes 1048576
  186.4 21.9 %all-to-all-start.3 = ((bf16[4,1,208,768]{3,2,1,0:T(8,128)(2,1)}), bf16[4,1,208,768]{3,2,1,0:T(8,128)(2,1)}, u32[]{:S(2)}, u32[]{:S(2)}) async-start(bf16[4,1,208,768]{3,2,1,0:T(8,128)(2,1)} %fusion.214), calls=%async_computation.3 | async-start | bytes 2555904 | tf_op jit(solution)/shard_map/all_to_all | solution.py:164
  208.4 21.4 %all-to-all-start.1 = ((bf16[4,1,208,768]{3,2,1,0:T(8,128)(2,1)}), bf16[4,1,208,768]{3,2,1,0:T(8,128)(2,1)}, u32[]{:S(2)}, u32[]{:S(2)}) async-start(bf16[4,1,208,768]{3,2,1,0:T(8,128)(2,1)} %fusion.219), calls=%async_computation.1 | async-start | bytes 2555904 | tf_op jit(solution)/shard_map/all_to_all | solution.py:164
  212.8 474.9 %reduce-scatter.28.cloned.1.call-start = ((), (), s32[]{:S(2)}) async-start(), calls=%async_computation.25 | async-start | bytes 5308416
  232.6 28.9 %slice-start.11 = ((s8[10223616]{0:T(1024)(128)(4,1)}), s8[4194304]{0:T(1024)(128)(4,1)S(1)}, s32[]{:S(2)}) async-start(s8[10223616]{0:T(1024)(128)(4,1)} %bitcast.669), calls=%async_computation.37 | async-start | bytes 8388608
  232.6 28.9 %slice-start.12 = ((s8[10223616]{0:T(1024)(128)(4,1)}), s8[4194304]{0:T(1024)(128)(4,1)S(1)}, s32[]{:S(2)}) async-start(s8[10223616]{0:T(1024)(128)(4,1)} %bitcast.669), calls=%async_computation.38 | async-start | bytes 8388608
  237.5 24.0 %slice-start.7 = ((s8[4718592]{0:T(1024)(128)(4,1)}), s8[4194304]{0:T(1024)(128)(4,1)S(1)}, s32[]{:S(2)}) async-start(s8[4718592]{0:T(1024)(128)(4,1)} %bitcast.663), calls=%async_computation.33 | async-start | bytes 8388608
  237.5 24.0 %slice-start.13 = ((s8[10223616]{0:T(1024)(128)(4,1)}), s8[1835008]{0:T(1024)(128)(4,1)S(1)}, s32[]{:S(2)}) async-start(s8[10223616]{0:T(1024)(128)(4,1)} %bitcast.669), calls=%async_computation.39 | async-start | bytes 3670016
  239.0 22.5 %slice-start.8 = ((s8[4718592]{0:T(1024)(128)(4,1)}), s8[524288]{0:T(1024)(128)(4,1)S(1)}, s32[]{:S(2)}) async-start(s8[4718592]{0:T(1024)(128)(4,1)} %bitcast.663), calls=%async_computation.34 | async-start | bytes 1048576
  308.6 382.5 %reduce-scatter.26.cloned.1.call-start = ((), (), s32[]{:S(2)}) async-start(), calls=%async_computation.24 | async-start | bytes 5308416
  309.1 25.6 %slice-start.9 = ((s8[4718592]{0:T(1024)(128)(4,1)}), s8[4194304]{0:T(1024)(128)(4,1)S(1)}, s32[]{:S(2)}) async-start(s8[4718592]{0:T(1024)(128)(4,1)} %bitcast.665), calls=%async_computation.35 | async-start | bytes 8388608
  311.9 22.8 %slice-start.10 = ((s8[4718592]{0:T(1024)(128)(4,1)}), s8[524288]{0:T(1024)(128)(4,1)S(1)}, s32[]{:S(2)}) async-start(s8[4718592]{0:T(1024)(128)(4,1)} %bitcast.665), calls=%async_computation.36 | async-start | bytes 1048576
  384.9 310.8 %reduce-scatter.14.cloned.1.call-start = ((), (), s32[]{:S(2)}) async-start(), calls=%async_computation.18 | async-start | bytes 5308416 | tf_op jit(solution)/shard_map/reduce_scatter | solution.py:306
  396.4 300.5 %reduce-scatter.16.cloned.1.call-start = ((), (), s32[]{:S(2)}) async-start(), calls=%async_computation.19 | async-start | bytes 5308416 | tf_op jit(solution)/shard_map/reduce_scatter | solution.py:306
  465.7 20.8 %all-to-all-start.5 = ((bf16[4,1,208,768]{3,2,1,0:T(8,128)(2,1)}), bf16[4,1,208,768]{3,2,1,0:T(8,128)(2,1)S(1)}, u32[]{:S(2)}, u32[]{:S(2)}) async-start(bf16[4,1,208,768]{3,2,1,0:T(8,128)(2,1)} %fusion.209), calls=%async_computation.5 | async-start | bytes 2555904 | tf_op jit(solution)/shard_map/all_to_all | solution.py:207
  486.5 21.3 %all-to-all-start.7 = ((bf16[4,1,208,768]{3,2,1,0:T(8,128)(2,1)}), bf16[4,1,208,768]{3,2,1,0:T(8,128)(2,1)}, u32[]{:S(2)}, u32[]{:S(2)}) async-start(bf16[4,1,208,768]{3,2,1,0:T(8,128)(2,1)} %fusion.204), calls=%async_computation.7 | async-start | bytes 2555904 | tf_op jit(solution)/shard_map/all_to_all | solution.py:207
  490.8 310.9 %reduce-scatter.24.cloned.1.call-start = ((), (), s32[]{:S(2)}) async-start(), calls=%async_computation.23 | async-start | bytes 2433024 | tf_op jit(solution)/shard_map/reduce_scatter | solution.py:295
  492.2 15.6 %copy-start.98 = (s32[6,512]{1,0:T(8,128)S(1)}, s32[6,512]{1,0:T(8,128)}, u32[]{:S(2)}) copy-start(s32[6,512]{1,0:T(8,128)} %copy-done.97) | copy-start | bytes 36868
  492.2 15.6 %copy-start.106 = (pred[6,512]{1,0:T(8,128)(4,1)S(1)}, pred[6,512]{1,0:T(8,128)(4,1)}, u32[]{:S(2)}) copy-start(pred[6,512]{1,0:T(8,128)(4,1)} %convert_compare_fusion) | copy-start | bytes 9220
  492.2 15.6 %copy-start.108 = (pred[6,512]{1,0:T(8,128)(4,1)S(1)}, pred[6,512]{1,0:T(8,128)(4,1)}, u32[]{:S(2)}) copy-start(pred[6,512]{1,0:T(8,128)(4,1)} %convert_compare_fusion.1) | copy-start | bytes 9220
  495.1 16.5 %copy-start.32 = (f32[512,768]{1,0:T(8,128)}, f32[512,768]{1,0:T(8,128)S(1)}, u32[]{:S(2)}) copy-start(f32[512,768]{1,0:T(8,128)S(1)} %bitcast_add_fusion.1) | copy-start | bytes 4718596
  556.5 350.0 %reduce-scatter.22.cloned.1.call-start = ((), (), s32[]{:S(2)}) async-start(), calls=%async_computation.22 | async-start | bytes 2433024 | tf_op jit(solution)/shard_map/reduce_scatter | solution.py:294
  582.4 428.2 %reduce-scatter.20.cloned.1.call-start = ((), (), s32[]{:S(2)}) async-start(), calls=%async_computation.21 | async-start | bytes 2433024 | tf_op jit(solution)/shard_map/reduce_scatter | solution.py:293
  605.7 509.5 %reduce-scatter.18.cloned.1.call-start = ((), (), s32[]{:S(2)}) async-start(), calls=%async_computation.20 | async-start | bytes 2433024 | tf_op jit(solution)/shard_map/reduce_scatter | solution.py:292
  627.6 53.6 %copy-start.34 = (bf16[1,512,768]{2,1,0:T(8,128)(2,1)S(1)}, bf16[1,512,768]{2,1,0:T(8,128)(2,1)}, u32[]{:S(2)}) copy-start(bf16[1,512,768]{2,1,0:T(8,128)(2,1)} %get-tuple-element.62) | copy-start | bytes 2359300
  (126 other events, 584.2 us)
Sparse Core Ops, SparseCore 0:
  10.1 83.6 all-gather.2
  96.0 78.0 all-gather.4
  308.7 92.4 reduce-scatter.27
  404.8 94.9 reduce-scatter.25
  503.3 94.9 reduce-scatter.13
  601.8 95.0 reduce-scatter.15
  702.8 98.8 reduce-scatter.23
  808.4 98.0 reduce-scatter.21
  912.4 98.1 reduce-scatter.19
  1017.1 98.0 reduce-scatter.17
where the time goes:
time: 1130 us; the launch traced here: 1120 us
  waiting for transfers between devices  483 us (43%)
  matrix products  341 us (30%)
  local copies, waits for them, and re-layouts  113 us (10%)
  blocking collectives  78.7 us (7%)
  other arithmetic  62.5 us (6%)
  starting transfers between devices  27.4 us (2%)
  between operations  16.2 us (1%)
    reduce_scatter x1, waiting for transfers between devices, per_device(): lax.psum_scatter(step_value, ('dp', 'expert'), scatter_dimension=0, tiled...  105 us
    reduce_scatter x1, waiting for transfers between devices, per_device(): lax.psum_scatter(step_query, ('dp', 'expert'), scatter_dimension=0, tiled...  105 us
    reduce_scatter x1, waiting for transfers between devices, per_device(): lax.psum_scatter(step_key, ('dp', 'expert'), scatter_dimension=0, tiled=T...  104 us
    reduce_scatter x1, waiting for transfers between devices, per_device(): lax.psum_scatter(step_output, ('dp', 'expert'), scatter_dimension=0, tile...  102 us
    unnamed x297, local copies, waits for them, and re-layouts  93.7 us
    all_to_all x2, blocking collectives, per_device(): lax.all_to_all(grad_sent, 'expert', split_axis=0, concat_axis=0, tiled=True)  39.4 us
    unnamed x1, blocking collectives  39.4 us
    all_gather x1, waiting for transfers between devices, per_device(): lax.all_gather(new_out.astype(half), 'dp', axis=1, tiled=True)  36.6 us
  transfers between devices with their start and end apart: 16, of which 9 were waited for; matrix products, arithmetic and copies ran while one was open for 39% of the time, Pallas kernels for 0%

commit v1 on v0

v1 whole, which is shorter than its diff:
```python
import functools

import jax
import jax.numpy as jnp
from jax import lax
from jax.experimental import pallas as pl
from jax.experimental.pallas import tpu as pltpu
from jax.sharding import PartitionSpec as P

HEAD = 64
PAIR = 2 * HEAD
TILE = 256
EPS = 1e-05
HALF = jnp.bfloat16
SINGLE = jnp.float32
HIDDEN = -1000000000.0
GELU_C = 0.7978845608028654
GELU_A = 0.044715

NN = (((1,), (0,)), ((), ()))
NT = (((1,), (1,)), ((), ()))
TN = (((0,), (0,)), ((), ()))


def mm(a, b, dims=NN):
    return lax.dot_general(a, b, dims, preferred_element_type=SINGLE)


def norm_rows(values):
    center = values - jnp.mean(values, -1, keepdims=True)
    inverse = lax.rsqrt(jnp.mean(center * center, -1, keepdims=True) + EPS)
    return center * inverse, inverse


def norm_back(grad, unit_rows, inverse, gain):
    scaled = grad * gain
    return inverse * (
        scaled
        - jnp.mean(scaled, -1, keepdims=True)
        - unit_rows * jnp.mean(scaled * unit_rows, -1, keepdims=True)
    )


def doc_of(places, ends_ref):
    doc = jnp.zeros(places.shape, jnp.int32)
    for i in range(ends_ref.shape[0]):
        doc = doc + jnp.where(places >= ends_ref[i], 1, 0)
    return doc


def half_masks(rows):
    lane = lax.broadcasted_iota(jnp.int32, (rows, PAIR), 1)
    first = jnp.where(lane < HEAD, 1.0, 0.0).astype(HALF)
    second = jnp.where(lane < HEAD, 0.0, 1.0).astype(HALF)
    return lane < HEAD, (first, second)


def route_hots(routes_t_ref, rows, tokens):
    sub = lax.broadcasted_iota(jnp.int32, (rows, tokens), 0)
    return [sub == routes_t_ref[pick : pick + 1, :] for pick in range(2)]


def attend_kernel(
    capacity,
    experts,
    frozen,
    ends_ref,
    x_ref,
    dy_ref,
    routes_t_ref,
    mask_ref,
    norms_ref,
    wq_ref,
    wk_ref,
    wv_ref,
    wo_ref,
    wr_ref,
    a1_ref,
    q_ref,
    k_ref,
    v_ref,
    o_ref,
    x1_ref,
    a2_ref,
    lse_ref,
    info_ref,
    cols_ref,
    probs_ref,
    froz_ref,
    send_ref,
    bias_scr,
    lse_scr,
):
    tokens, width = x_ref.shape
    chunk = 128
    gain_one, bias_one = norms_ref[0:1, :], norms_ref[1:2, :]
    gain_two, bias_two = norms_ref[2:3, :], norms_ref[3:4, :]

    @pl.loop(0, tokens // chunk)
    def _(i):
        rows = pl.ds(pl.multiple_of(i * chunk, chunk), chunk)
        unit_rows, _ = norm_rows(x_ref[rows, :].astype(SINGLE))
        a1_ref[rows, :] = (unit_rows * gain_one + bias_one).astype(HALF)
        here = lax.broadcasted_iota(jnp.int32, (chunk, 1), 0) + i * chunk
        there = lax.broadcasted_iota(jnp.int32, (1, tokens), 1)
        same = doc_of(here, ends_ref) == doc_of(there, ends_ref)
        keep = (mask_ref[...] == 1) | (there == here)
        visible = same & (there <= here) & keep
        bias_scr[rows, :] = jnp.where(visible, 0.0, HIDDEN)

    @pl.loop(0, tokens // TILE)
    def _(i):
        rows = pl.ds(pl.multiple_of(i * TILE, TILE), TILE)
        a1 = a1_ref[rows, :]
        q_ref[rows, :] = (mm(a1, wq_ref[...]).astype(HALF) * HEAD ** (-0.5)).astype(HALF)
        k_ref[rows, :] = mm(a1, wk_ref[...]).astype(HALF)
        v_ref[rows, :] = mm(a1, wv_ref[...]).astype(HALF)

    lse_scr[...] = jnp.zeros_like(lse_scr)

    @pl.loop(0, width // PAIR)
    def _(i):
        cols = pl.ds(pl.multiple_of(i * PAIR, PAIR), PAIR)
        low, masks = half_masks(TILE)
        lane = lax.broadcasted_iota(jnp.int32, (TILE, 128), 1)
        for part in range(tokens // TILE):
            rows = slice(part * TILE, (part + 1) * TILE)
            keys = (part + 1) * TILE
            q_t = q_ref[rows, cols]
            k_t = k_ref[0:keys, cols]
            v_t = v_ref[0:keys, cols]
            results = []
            for h in range(2):
                scores = mm(q_t * masks[h], k_t, NT) + bias_scr[rows, 0:keys]
                top = jnp.max(scores, -1, keepdims=True)
                expo = jnp.exp(scores - top)
                total = jnp.sum(expo, -1, keepdims=True)
                results.append(mm(expo.astype(HALF), v_t) * (1.0 / total))
                log_total = top + jnp.log(total)
                lse_scr[rows, :] = jnp.where(lane == 2 * i + h, log_total, lse_scr[rows, :])
            o_ref[rows, cols] = jnp.where(low, results[0], results[1]).astype(HALF)

    lse_ref[...] = jnp.transpose(lse_scr[...])[0 : lse_ref.shape[0], :]

    @pl.loop(0, tokens // TILE)
    def _(i):
        rows = pl.ds(pl.multiple_of(i * TILE, TILE), TILE)
        x1 = x_ref[rows, :].astype(SINGLE) + mm(o_ref[rows, :], wo_ref[...])
        x1_ref[rows, :] = x1
        unit_rows, _ = norm_rows(x1)
        a2_ref[rows, :] = (unit_rows * gain_two + bias_two).astype(HALF)

    rows16 = wr_ref.shape[0]
    logits = mm(wr_ref[...], a2_ref[...], NT)
    sub = lax.broadcasted_iota(jnp.int32, (rows16, tokens), 0)
    logits = jnp.where(sub < experts, logits, -1e30)
    expo = jnp.exp(logits - jnp.max(logits, 0, keepdims=True))
    probs = expo / jnp.sum(expo, 0, keepdims=True)
    probs_ref[...] = probs
    hots = route_hots(routes_t_ref, rows16, tokens)
    chosen = [jnp.sum(jnp.where(hot, probs, 0.0), 0, keepdims=True) for hot in hots]
    chosen_total = chosen[0] + chosen[1]
    gates = [one / chosen_total for one in chosen]
    upper = jnp.where(
        lax.broadcasted_iota(jnp.int32, (tokens, tokens), 0)
        < lax.broadcasted_iota(jnp.int32, (tokens, tokens), 1),
        1.0,
        0.0,
    ).astype(HALF)
    both = jnp.where(hots[0] | hots[1], 1.0, 0.0).astype(HALF)
    earlier = mm(both, upper)
    places = []
    for pick in range(2):
        slot = jnp.sum(jnp.where(hots[pick], earlier, 0.0), 0, keepdims=True)
        first = routes_t_ref[pick : pick + 1, :].astype(SINGLE) * capacity
        places.append(jnp.where(slot < capacity, first + slot, -1.0))
    info = jnp.concatenate(
        places + gates + [mask_ref[...].astype(SINGLE), chosen_total, chosen_total, chosen_total], 0
    )
    info_ref[...] = info
    cols_ref[...] = jnp.transpose(
        jnp.concatenate([info, jnp.zeros((128 - info.shape[0], tokens), SINGLE)], 0)
    )
    spots = [one.astype(jnp.int32) for one in places]
    for e in range(experts):
        slots = lax.broadcasted_iota(jnp.int32, (capacity, tokens), 0) + e * capacity
        hit = [slots == spots[pick] for pick in range(2)]
        place = jnp.where(hit[0] | hit[1], 1.0, 0.0).astype(HALF)
        weight = jnp.sum(
            jnp.where(hit[0], gates[0], 0.0) + jnp.where(hit[1], gates[1], 0.0), 1, keepdims=True
        )
        target = froz_ref.at[e] if e < frozen else send_ref.at[e - frozen]
        target[0] = mm(place, a2_ref[...]).astype(HALF)
        target[1] = (mm(place, dy_ref[...]) * weight).astype(HALF)


def expert_step(x_scr, dy_scr, w_in, w_out, in_dims, acc_scr, h_scr, dp_scr, first, chunk):
    back_dims = NT if in_dims == NN else NN

    @pl.loop(0, x_scr.shape[0] // chunk)
    def _(i):
        rows = pl.ds(pl.multiple_of(i * chunk, 16), chunk)
        pre = mm(x_scr[rows, :], w_in, in_dims)
        grad = mm(dy_scr[rows, :], w_out, NT)
        square = pre * pre
        tanh = jnp.tanh(GELU_C * pre * (1.0 + GELU_A * square))
        plus = 0.5 * (1.0 + tanh)
        hidden = (pre * plus).astype(HALF)
        slope = plus + 0.5 * pre * (1.0 - tanh * tanh) * (GELU_C * (1.0 + 3.0 * GELU_A * square))
        grad_pre = (grad * slope).astype(HALF)
        if h_scr is not None:
            h_scr[rows, :] = hidden
            dp_scr[rows, :] = grad_pre
        out = mm(hidden, w_out)
        back = mm(grad_pre, w_in, back_dims)

        @pl.when(first)
        def _():
            acc_scr[0, rows, :] = out
            acc_scr[1, rows, :] = back

        @pl.when(jnp.logical_not(first))
        def _():
            acc_scr[0, rows, :] += out
            acc_scr[1, rows, :] += back


def frozen_kernel(
    r0_ref, r1_ref, win_ref, wout_ref, o0_ref, o1_ref, x_scr, dy_scr, acc_scr
):
    capacity = r0_ref.shape[2]
    step, last = pl.program_id(1), pl.num_programs(1) - 1

    @pl.when(step == 0)
    def _():
        for m, ref in enumerate((r0_ref, r1_ref)):
            x_scr[m * capacity : (m + 1) * capacity, :] = ref[0, 0]
            dy_scr[m * capacity : (m + 1) * capacity, :] = ref[0, 1]

    expert_step(
        x_scr, dy_scr, win_ref[0], wout_ref[0], NN, acc_scr, None, None, step == 0, capacity
    )

    @pl.when(step == last)
    def _():
        for m, ref in enumerate((o0_ref, o1_ref)):
            for part in range(2):
                ref[0, part] = acc_scr[part, m * capacity : (m + 1) * capacity, :].astype(HALF)


def owned_kernel(
    r0_ref,
    r1_ref,
    w_ref,
    o0_ref,
    o1_ref,
    dw_ref,
    x_scr,
    dy_scr,
    xt_scr,
    dyt_scr,
    acc_scr,
    h_scr,
    dp_scr,
):
    sources, _, capacity, width = r0_ref.shape
    group, _, shard, _ = w_ref.shape
    step, last = pl.program_id(0), pl.num_programs(0) - 1
    rows_all = x_scr.shape[0]

    @pl.when(step == 0)
    def _():
        for m, ref in enumerate((r0_ref, r1_ref)):
            for s in range(sources):
                at = (m * sources + s) * capacity
                x_scr[at : at + capacity, :] = ref[s, 0]
                dy_scr[at : at + capacity, :] = ref[s, 1]
        for at in range(0, width, 128):
            xt_scr[at : at + 128, :] = jnp.transpose(x_scr[:, at : at + 128])
            dyt_scr[at : at + 128, :] = jnp.transpose(dy_scr[:, at : at + 128])

    w_in = w_ref[:, 0].reshape(group * shard, width)
    w_out = w_ref[:, 1].reshape(group * shard, width)
    expert_step(
        x_scr, dy_scr, w_in, w_out, NT, acc_scr, h_scr, dp_scr, step == 0, 2 * capacity
    )

    @pl.loop(0, width // TILE)
    def _(i):
        rows = pl.ds(pl.multiple_of(i * TILE, TILE), TILE)
        for part, (left, right) in enumerate(((xt_scr, dp_scr), (dyt_scr, h_scr))):
            total = mm(left[rows, :], right[...]).astype(HALF)
            for g in range(group):
                dw_ref[g, part, rows, :] = total[:, g * shard : (g + 1) * shard]

    @pl.when(step == last)
    def _():
        for m, ref in enumerate((o0_ref, o1_ref)):
            for s in range(sources):
                at = (m * sources + s) * capacity
                for part in range(2):
                    ref[s, part] = acc_scr[part, at : at + capacity, :].astype(HALF)


def back_kernel(
    capacity,
    experts,
    ends_ref,
    x_ref,
    dy_ref,
    routes_t_ref,
    norms_ref,
    wq_ref,
    wk_ref,
    wv_ref,
    wo_ref,
    wr_ref,
    q_ref,
    k_ref,
    v_ref,
    o_ref,
    x1_ref,
    a2_ref,
    lse_ref,
    info_ref,
    cols_ref,
    probs_ref,
    froz_ref,
    back_ref,
    mixed_ref,
    xgrad_ref,
    dq_ref,
    dk_ref,
    dv_ref,
    db_ref,
    small_ref,
    out_scr,
    dbuf_scr,
    bias_scr,
    dx1_scr,
    do_scr,
    delta_scr,
):
    tokens, width = x_ref.shape
    frozen = froz_ref.shape[0]
    gain_one, gain_two = norms_ref[0:1, :], norms_ref[2:3, :]
    slots_all = experts * capacity
    for e in range(experts):
        source = froz_ref.at[e] if e < frozen else back_ref.at[e - frozen]
        out_scr[e * capacity : (e + 1) * capacity, :] = source[0]
        dbuf_scr[e * capacity : (e + 1) * capacity, :] = source[1]

    spots = [info_ref[pick : pick + 1, :].astype(jnp.int32) for pick in range(2)]
    gates = [info_ref[2 + pick : 3 + pick, :] for pick in range(2)]
    chosen_total = info_ref[5:6, :]

    def gate_part(e, carry):
        rows = pl.ds(pl.multiple_of(e * capacity, 16), capacity)
        overlap = mm(out_scr[rows, :], dy_ref[...], NT)
        slots = lax.broadcasted_iota(jnp.int32, (capacity, tokens), 0) + e * capacity
        return tuple(
            carry[pick]
            + jnp.sum(jnp.where(slots == spots[pick], overlap, 0.0), 0, keepdims=True)
            for pick in range(2)
        )

    zero_row = jnp.zeros((1, tokens), SINGLE)
    gate_grads = lax.fori_loop(0, experts, gate_part, (zero_row, zero_row))
    rows16 = wr_ref.shape[0]
    hots = route_hots(routes_t_ref, rows16, tokens)
    weighted = gate_grads[0] * gates[0] + gate_grads[1] * gates[1]
    grad_probs = jnp.where(hots[0], (gate_grads[0] - weighted) / chosen_total, 0.0)
    grad_probs = grad_probs + jnp.where(hots[1], (gate_grads[1] - weighted) / chosen_total, 0.0)
    probs = probs_ref[...]
    grad_logits = probs * (grad_probs - jnp.sum(grad_probs * probs, 0, keepdims=True))
    logits_low = grad_logits.astype(HALF)
    small_ref[0:rows16, :] = mm(logits_low, a2_ref[...])
    small_ref[rows16:, :] = jnp.zeros_like(small_ref[rows16:, :])

    @pl.loop(0, tokens // TILE)
    def _(i):
        rows = pl.ds(pl.multiple_of(i * TILE, TILE), TILE)
        slots = lax.broadcasted_iota(jnp.int32, (TILE, slots_all), 1)
        hit = [slots == cols_ref[rows, pick : pick + 1].astype(jnp.int32) for pick in range(2)]
        gated = jnp.where(hit[0], cols_ref[rows, 2:3], 0.0)
        gated = jnp.where(hit[1], cols_ref[rows, 3:4], gated).astype(HALF)
        place = jnp.where(hit[0] | hit[1], 1.0, 0.0).astype(HALF)
        x1 = x1_ref[rows, :]
        mixed_ref[rows, :] = (x1 + mm(gated, out_scr[...])).astype(HALF)
        dx1_scr[rows, :] = mm(place, dbuf_scr[...])

    logits_col = jnp.transpose(
        jnp.concatenate([grad_logits, jnp.zeros((128 - rows16, tokens), SINGLE)], 0)
    )
    delta_scr[...] = logits_col.astype(HALF).astype(SINGLE)
    router = jnp.concatenate([wr_ref[...], jnp.zeros((128 - rows16, width), HALF)], 0)

    @pl.loop(0, tokens // TILE)
    def _(i):
        rows = pl.ds(pl.multiple_of(i * TILE, TILE), TILE)
        unit_rows, inverse = norm_rows(x1_ref[rows, :])
        grad = dx1_scr[rows, :] + mm(delta_scr[rows, :].astype(HALF), router)
        small_ref[rows16 : rows16 + 1, :] += jnp.sum(grad * unit_rows, 0, keepdims=True)
        small_ref[rows16 + 1 : rows16 + 2, :] += jnp.sum(grad, 0, keepdims=True)
        dx1 = dy_ref[rows, :].astype(SINGLE) + norm_back(grad, unit_rows, inverse, gain_two)
        dx1_scr[rows, :] = dx1
        branch = dx1.astype(HALF)
        db_ref[rows, :] = branch
        do_scr[rows, :] = mm(branch, wo_ref[...], NT).astype(HALF)

    @pl.loop(0, tokens // 128)
    def _(i):
        rows = pl.ds(pl.multiple_of(i * 128, 128), 128)
        key = lax.broadcasted_iota(jnp.int32, (128, 1), 0) + i * 128
        query = lax.broadcasted_iota(jnp.int32, (1, tokens), 1)
        same = doc_of(key, ends_ref) == doc_of(query, ends_ref)
        keep = (cols_ref[rows, 4:5] > 0.5) | (query == key)
        visible = same & (key <= query) & keep
        bias_scr[rows, :] = jnp.where(visible, 0.0, HIDDEN)

    @pl.loop(0, width // PAIR)
    def _(i):
        cols = pl.ds(pl.multiple_of(i * PAIR, PAIR), PAIR)
        low, masks = half_masks(TILE)
        tiles = tokens // TILE
        half_sum = jnp.where(
            (lax.broadcasted_iota(jnp.int32, (8, PAIR), 1) // HEAD)
            == lax.broadcasted_iota(jnp.int32, (8, PAIR), 0),
            1.0,
            0.0,
        )
        overlap = do_scr[:, cols].astype(SINGLE) * o_ref[:, cols].astype(SINGLE)
        deltas = lax.dot_general(
            half_sum,
            overlap,
            NT,
            precision=lax.Precision.HIGHEST,
            preferred_element_type=SINGLE,
        )
        grad_q = [[None] * tiles for _ in range(2)]
        for part in range(tiles):
            keys = slice(part * TILE, (part + 1) * TILE)
            queries = slice(part * TILE, tokens)
            k_t, v_t = k_ref[keys, cols], v_ref[keys, cols]
            q_t, do_t = q_ref[queries, cols], do_scr[queries, cols]
            grad_k, grad_v = [], []
            for h in range(2):
                scores = mm(k_t * masks[h], q_t, NT) + bias_scr[keys, queries]
                log_total = lse_ref[pl.ds(2 * i + h, 1), queries]
                probs = jnp.exp(scores - log_total)
                grad_p = mm(v_t * masks[h], do_t, NT)
                grad_s = (probs * (grad_p - deltas[h : h + 1, queries])).astype(HALF)
                grad_v.append(mm(probs.astype(HALF), do_t))
                grad_k.append(mm(grad_s, q_t))
                step = mm(grad_s, k_t, TN)
                for t in range(part, tiles):
                    piece = step[(t - part) * TILE : (t - part + 1) * TILE, :]
                    grad_q[h][t] = piece if grad_q[h][t] is None else grad_q[h][t] + piece
            dv_ref[keys, cols] = jnp.where(low, grad_v[0], grad_v[1]).astype(HALF)
            dk_ref[keys, cols] = jnp.where(low, grad_k[0], grad_k[1]).astype(HALF)
        for t in range(tiles):
            both = jnp.where(low, grad_q[0][t], grad_q[1][t]) * HEAD ** (-0.5)
            dq_ref[t * TILE : (t + 1) * TILE, cols] = both.astype(HALF)

    @pl.loop(0, tokens // TILE)
    def _(i):
        rows = pl.ds(pl.multiple_of(i * TILE, TILE), TILE)
        unit_rows, inverse = norm_rows(x_ref[rows, :].astype(SINGLE))
        grad = mm(dq_ref[rows, :], wq_ref[...], NT)
        grad = grad + mm(dk_ref[rows, :], wk_ref[...], NT)
        grad = grad + mm(dv_ref[rows, :], wv_ref[...], NT)
        small_ref[rows16 + 2 : rows16 + 3, :] += jnp.sum(grad * unit_rows, 0, keepdims=True)
        small_ref[rows16 + 3 : rows16 + 4, :] += jnp.sum(grad, 0, keepdims=True)
        part = norm_back(grad, unit_rows, inverse, gain_one)
        xgrad_ref[rows, :] = (dx1_scr[rows, :] + part).astype(HALF)


def weights_kernel(*refs):
    ins, dw_ref = refs[:-1], refs[-1]
    micro = len(ins) // 6
    width = dw_ref.shape[-1]

    @pl.loop(0, width // TILE)
    def _(i):
        cols = pl.ds(pl.multiple_of(i * TILE, TILE), TILE)
        for part in range(4):
            total = None
            for m in range(micro):
                a1, o, dq, dk, dv, db = ins[6 * m : 6 * m + 6]
                left = o if part == 3 else a1
                right = (dq, dk, dv, db)[part]
                step = mm(left[:, cols], right[...], TN)
                total = step if total is None else total + step
            dw_ref[part, cols, :] = total.astype(HALF)


def vmem(count):
    return [pl.BlockSpec(memory_space=pltpu.VMEM)] * count


def params(mib, **more):
    return pltpu.CompilerParams(vmem_limit_bytes=mib << 20, **more)


def per_device(
    tokens,
    routes,
    lengths,
    key_mask,
    gain_one,
    bias_one,
    w_query,
    w_key,
    w_value,
    w_output,
    gain_two,
    bias_two,
    w_router,
    frozen_in,
    frozen_out,
    new_in,
    new_out,
    cotangent,
):
    micro, tok, width = tokens.shape
    owners = lax.axis_size("expert")
    dp = lax.axis_size("dp")
    frozen, _, ff = frozen_in.shape
    experts = frozen + owners
    capacity = 10 * tok // (4 * experts) // 8 * 8
    shard = new_in.shape[2]
    slots_all = experts * capacity
    shape = jax.ShapeDtypeStruct
    smem = pl.BlockSpec(memory_space=pltpu.SMEM)

    local_w = jnp.stack([new_in[0].T.astype(HALF), new_out[0].astype(HALF)], 0)
    all_w = lax.all_gather(local_w, "dp", axis=0, tiled=False)

    ends = jnp.cumsum(lengths[:, 0], axis=1).astype(jnp.int32)
    routes_t = jnp.swapaxes(routes, 1, 2)
    norms = jnp.stack([gain_one, bias_one, gain_two, bias_two], 0)
    rows16 = 16
    router_t = jnp.zeros((rows16, width), HALF).at[:experts].set(w_router.T)

    saved, froz_sent, arrived = [], [], []
    for m in range(micro):
        outs = pl.pallas_call(
            functools.partial(attend_kernel, capacity, experts, frozen),
            out_shape=[shape((tok, width), HALF)] * 5
            + [
                shape((tok, width), SINGLE),
                shape((tok, width), HALF),
                shape((16, tok), SINGLE),
                shape((8, tok), SINGLE),
                shape((tok, 128), SINGLE),
                shape((rows16, tok), SINGLE),
                shape((frozen, 2, capacity, width), HALF),
                shape((owners, 2, capacity, width), HALF),
            ],
            in_specs=[smem] + vmem(10),
            out_specs=vmem(13),
            scratch_shapes=[pltpu.VMEM((tok, tok), SINGLE), pltpu.VMEM((tok, 128), SINGLE)],
            compiler_params=params(56),
            cost_estimate=pl.CostEstimate(
                flops=8_000_000_000, bytes_accessed=20_000_000, transcendentals=3_000_000
            ),
            name="attend",
        )(
            ends[m],
            tokens[m],
            cotangent[m],
            routes_t[m],
            key_mask[m][None, :],
            norms,
            w_query,
            w_key,
            w_value,
            w_output,
            router_t,
        )
        saved.append(outs[:11])
        froz_sent.append(outs[11])
        arrived.append(
            lax.all_to_all(outs[12], "expert", split_axis=0, concat_axis=0, tiled=True)
        )

    block = min(768, ff)
    rows_spec = pl.BlockSpec((1, 2, capacity, width), lambda e, f: (e, 0, 0, 0))
    froz_back = pl.pallas_call(
        frozen_kernel,
        grid=(frozen, ff // block),
        out_shape=[shape((frozen, 2, capacity, width), HALF)] * 2,
        in_specs=[
            rows_spec,
            rows_spec,
            pl.BlockSpec((1, width, block), lambda e, f: (e, 0, f)),
            pl.BlockSpec((1, block, width), lambda e, f: (e, f, 0)),
        ],
        out_specs=[rows_spec, rows_spec],
        scratch_shapes=[
            pltpu.VMEM((2 * capacity, width), HALF),
            pltpu.VMEM((2 * capacity, width), HALF),
            pltpu.VMEM((2, 2 * capacity, width), SINGLE),
        ],
        compiler_params=params(50),
        cost_estimate=pl.CostEstimate(
            flops=16_000_000_000, bytes_accessed=25_000_000, transcendentals=2_500_000
        ),
        name="frozen",
    )(froz_sent[0], froz_sent[1], frozen_in, frozen_out)

    rows_all = micro * owners * capacity
    group = max(1, 768 // shard)
    whole = pl.BlockSpec((owners, 2, capacity, width), lambda f: (0, 0, 0, 0))
    done0, done1, grads_w = pl.pallas_call(
        owned_kernel,
        grid=(dp // group,),
        out_shape=[shape((owners, 2, capacity, width), HALF)] * 2
        + [shape((dp, 2, width, shard), HALF)],
        in_specs=[whole, whole, pl.BlockSpec((group, 2, shard, width), lambda f: (f, 0, 0, 0))],
        out_specs=[whole, whole, pl.BlockSpec((group, 2, width, shard), lambda f: (f, 0, 0, 0))],
        scratch_shapes=[
            pltpu.VMEM((rows_all, width), HALF),
            pltpu.VMEM((rows_all, width), HALF),
            pltpu.VMEM((width, rows_all), HALF),
            pltpu.VMEM((width, rows_all), HALF),
            pltpu.VMEM((2, rows_all, width), SINGLE),
            pltpu.VMEM((rows_all, group * shard), HALF),
            pltpu.VMEM((rows_all, group * shard), HALF),
        ],
        compiler_params=params(60),
        cost_estimate=pl.CostEstimate(
            flops=47_000_000_000, bytes_accessed=35_000_000, transcendentals=5_000_000
        ),
        name="owned",
    )(arrived[0], arrived[1], all_w)

    returned = [
        lax.all_to_all(one, "expert", split_axis=0, concat_axis=0, tiled=True)
        for one in (done0, done1)
    ]
    summed_w = lax.psum_scatter(grads_w, "dp", scatter_dimension=0, tiled=True)[0]

    mixed_list, xgrad_list, small_list, weight_ins = [], [], [], []
    for m in range(micro):
        a1, q, k, v, o, x1, a2, lse, info, cols, probs = saved[m]
        mixed, xgrad, dq, dk, dv, db, small = pl.pallas_call(
            functools.partial(back_kernel, capacity, experts),
            out_shape=[shape((tok, width), HALF)] * 6 + [shape((rows16 + 8, width), SINGLE)],
            in_specs=[smem] + vmem(21),
            out_specs=vmem(7),
            scratch_shapes=[
                pltpu.VMEM((slots_all, width), HALF),
                pltpu.VMEM((slots_all, width), HALF),
                pltpu.VMEM((tok, tok), SINGLE),
                pltpu.VMEM((tok, width), SINGLE),
                pltpu.VMEM((tok, width), HALF),
                pltpu.VMEM((tok, 128), SINGLE),
            ],
            compiler_params=params(56),
            cost_estimate=pl.CostEstimate(
                flops=16_000_000_000, bytes_accessed=25_000_000, transcendentals=3_000_000
            ),
            name="back",
        )(
            ends[m],
            tokens[m],
            cotangent[m],
            routes_t[m],
            norms,
            w_query,
            w_key,
            w_value,
            w_output,
            router_t,
            q,
            k,
            v,
            o,
            x1,
            a2,
            lse,
            info,
            cols,
            probs,
            froz_back[m],
            returned[m],
        )
        mixed_list.append(mixed)
        xgrad_list.append(xgrad)
        small_list.append(small)
        weight_ins += [a1, o, dq, dk, dv, db]

    grads = pl.pallas_call(
        weights_kernel,
        out_shape=shape((4, width, width), HALF),
        in_specs=vmem(len(weight_ins)),
        out_specs=vmem(1)[0],
        compiler_params=params(50),
        name="weights",
    )(*weight_ins)
    shared = lax.psum_scatter(grads, ("dp", "expert"), scatter_dimension=1, tiled=True)
    small = sum(small_list[1:], small_list[0])
    small = jnp.concatenate([small[:experts], small[rows16 : rows16 + 4]], 0).T
    small = lax.psum_scatter(small, ("dp", "expert"), scatter_dimension=0, tiled=True)
    shared = shared.astype(SINGLE)
    return (
        jnp.stack(mixed_list, 0),
        jnp.stack(xgrad_list, 0),
        small[:, experts + 2],
        small[:, experts + 3],
        shared[0],
        shared[1],
        shared[2],
        shared[3],
        small[:, experts],
        small[:, experts + 1],
        small[:, :experts],
        summed_w[0].astype(SINGLE)[None],
        summed_w[1].astype(SINGLE).T[None],
    )


def solution(mesh):
    both = ("dp", "expert")
    return jax.shard_map(
        per_device,
        mesh=mesh,
        in_specs=(
            P(None, both, None),
            P(None, both, None),
            P(None, both, None),
            P(None, both),
        )
        + (P(),) * 11
        + (P("expert", None, "dp"), P("expert", "dp", None), P(None, both, None)),
        out_specs=(P(None, both, None), P(None, both, None), P(both), P(both))
        + (P(both, None),) * 4
        + (P(both), P(both), P(both, None), P("expert", None, "dp"), P("expert", "dp", None)),
        check_vma=False,
    )
```

time: 1130 us -> 657 us (0.58)
  matrix products: 341 us -> 0 us
  Pallas kernels: 0 us -> 207 us
  waiting for transfers between devices: 483 us -> 280 us
  local copies, waits for them, and re-layouts: 113 us -> 23.8 us
  other arithmetic: 62.5 us -> 6.98 us
  blocking collectives: 78.7 us -> 110 us
  starting transfers between devices: 27.4 us -> 9.41 us
    dot_general x74 -> x0, matrix products: 341 us -> none  [the longest x2 25.6 us: per_device(): jnp.einsum('ecf,edf->ecd', grad_frozen_pre, frozen_in, preferred_element_...]
    reduce_scatter x6 -> x1, waiting for transfers between devices: 417 us -> 165 us  [per_device(): lax.psum_scatter(grads_w, 'dp', scatter_dimension=0, tiled=True)[0]]
    pallas_call x0 -> x7, Pallas kernels: none -> 207 us  [the longest x1 68.2 us: per_device(): pl.pallas_call(owned_kernel, grid=(dp // group,), out_shape=[shape((owner...]
    unnamed x297 -> x55, local copies, waits for them, and re-layouts: 93.7 us -> 16.3 us
    unnamed x12 -> x4, waiting for transfers between devices: 0.19 us -> 61.6 us
    all_to_all x2, blocking collectives: 39.4 us -> 70.3 us  [the longest x1 35.1 us: per_device(): lax.all_to_all(outs[12], 'expert', split_axis=0, concat_axis=0, tiled=True)]
    convert_element_type x5 -> x2, other arithmetic: 22.8 us -> 0.08 us  [the longest x1 0.06 us: per_device(): local_w = jnp.stack([new_in[0].T.astype(HALF), new_out[0].astype(HALF)], 0)]
    all_to_all x6 -> x2, waiting for transfers between devices: 29.3 us -> 9.72 us  [the longest x1 9.72 us: per_device(): lax.all_to_all(outs[12], 'expert', split_axis=0, concat_axis=0, tiled=True)]
  transfers between devices with their start and end apart: 16 -> 5, of which waited for: 9 -> 4; matrix products, arithmetic and copies ran while one was open for 39% -> 2% of each run, Pallas kernels for 0% -> 15%
where the time goes in v1:
time: 657 us; the launch traced here: 651 us
  waiting for transfers between devices  280 us (43%)
  Pallas kernels  207 us (32%)
  blocking collectives  110 us (17%)
  local copies, waits for them, and re-layouts  23.8 us (4%)
  between operations  14.6 us (2%)
  starting transfers between devices  9.41 us (1%)
  other arithmetic  6.98 us (1%)
    reduce_scatter x1, waiting for transfers between devices, per_device(): lax.psum_scatter(grads_w, 'dp', scatter_dimension=0, tiled=True)[0]  165 us
    pallas_call x1, Pallas kernels, per_device(): pl.pallas_call(owned_kernel, grid=(dp // group,), out_shape=[shape((owner...  68.2 us
    unnamed x4, waiting for transfers between devices  61.6 us
    pallas_call x2, Pallas kernels, per_device(): pl.pallas_call(functools.partial(back_kernel, capacity, experts), out_sha...  57.6 us
    all_gather x1, waiting for transfers between devices, per_device(): all_w = lax.all_gather(local_w, 'dp', axis=0, tiled=False)  44.1 us
    pallas_call x2, Pallas kernels, per_device(): pl.pallas_call(functools.partial(attend_kernel, capacity, experts, frozen...  41.7 us
    unnamed x1, blocking collectives  39.3 us
    all_to_all x1, blocking collectives, per_device(): lax.all_to_all(outs[12], 'expert', split_axis=0, concat_axis=0, tiled=True)  35.1 us
  transfers between devices with their start and end apart: 5, of which 4 were waited for; matrix products, arithmetic and copies ran while one was open for 2% of the time, Pallas kernels for 15%

profile of v1, /device:TPU:0, one launch (start us, length us, event | category | flops | bytes accessed | tf_op | source)
XLA Modules:
  0.0 651.3 jit_solution(9047355112319690610)
XLA Ops:
  7.2 1.6 copy.33
  9.0 1.1 pad_maximum_fusion.2
  13.4 3.1 slice_bitcast_fusion.2
  16.5 20.8 %attend.2 = (bf16[512,768]{1,0:T(8,128)(2,1)}, bf16[512,768]{1,0:T(8,128)(2,1)}, bf16[512,768]{1,0:T(8,128)(2,1)}, bf16[512,768]{1,0:T(8,128)(2,1)}, bf16[512,76...) custom-call(s32[4]{0:T(128)} %get-tuple-element.159.ends_ref, ...), custom_call_target="tpu_custom_call" | custom-call | flops 8000000000 | bytes 20000000 | tf_op jit(solution)/shard_map/attend/pallas_call | solution.py:547
  37.3 4.4 all-to-all-start
  41.8 20.9 %attend.3 = (bf16[512,768]{1,0:T(8,128)(2,1)}, bf16[512,768]{1,0:T(8,128)(2,1)}, bf16[512,768]{1,0:T(8,128)(2,1)}, bf16[512,768]{1,0:T(8,128)(2,1)}, bf16[512,76...) custom-call(s32[4]{0:T(128)} %get-tuple-element.160.ends_ref, ...), custom_call_target="tpu_custom_call" | custom-call | flops 8000000000 | bytes 20000000 | tf_op jit(solution)/shard_map/attend/pallas_call | solution.py:547
  62.7 9.7 %all-to-all-done.r0_ref = bf16[4,2,208,768]{3,2,1,0:T(8,128)(2,1)S(1)} async-done(((bf16[4,2,208,768]{3,2,1,0:T(8,128)(2,1)}), bf16[4,2,208,768]{3,2,1,0:T(8,128)(2,1)S(1)}, u32[]{:S(2)}, u32[]{:S(2)}) %all-to-all-start) | async-done | bytes 2555936 | tf_op jit(solution)/shard_map/all_to_all | solution.py:584
  72.4 35.1 %all_to_all.20.r1_ref = bf16[4,2,208,768]{3,2,1,0:T(8,128)(2,1)} all-to-all(bf16[4,2,208,768]{3,2,1,0:T(8,128)(2,1)} %get-tuple-element.84), channel_id=1, replica_groups=mesh['dp'=8,'expert'=4] {'expert'}, dimensions={0} | all-to-all | bytes 5111808 | tf_op jit(solution)/shard_map/all_to_all | solution.py:584
  107.5 44.1 %all-gather.3.cloned.1.call-done = bf16[16,384,768]{2,1,0:T(8,128)(2,1)} async-done(((bf16[2,384,768]{2,1,0:T(8,128)(2,1)}), bf16[16,384,768]{2,1,0:T(8,128)(2,1)}) %all-gather.3.cloned.1.call-update) | async-done | bytes 9437200 | tf_op jit(solution)/shard_map/all_gather | solution.py:537
  151.6 68.2 %owned.1 = (bf16[4,2,208,768]{3,2,1,0:T(8,128)(2,1)}, bf16[4,2,208,768]{3,2,1,0:T(8,128)(2,1)}, bf16[8,2,768,384]{3,2,1,0:T(8,128)(2,1)}) custom-call(bf16[4,2,208,768]{3,2,1,0:T(8,128)(2,1)} %copy-done.8, bf16[4,2,208,768]{3,2,1,0:T(8,128)(2,1)} %all_to_all.20.r1_ref, bf16[8,2,384,768]{3,2,1,0:T(8,128)(2,1)} %bitcast.80), custom_call_target="tpu_custom_call" | custom-call | flops 46999998464 | bytes 35000000 | tf_op jit(solution)/shard_map/owned/pallas_call | solution.py:615
  219.8 35.1 %all_to_all.21.back_ref = bf16[4,2,208,768]{3,2,1,0:T(8,128)(2,1)} all-to-all(bf16[4,2,208,768]{3,2,1,0:T(8,128)(2,1)} %get-tuple-element.85), channel_id=1, replica_groups=mesh['dp'=8,'expert'=4] {'expert'}, dimensions={0} | all-to-all | bytes 5111808 | tf_op jit(solution)/shard_map/all_to_all | solution.py:639
  254.9 4.7 all-to-all-start.3
  259.8 28.9 %frozen.1 = (bf16[2,2,208,768]{3,2,1,0:T(8,128)(2,1)S(1)}, bf16[2,2,208,768]{3,2,1,0:T(8,128)(2,1)S(1)}) custom-call(bf16[2,2,208,768]{3,2,1,0:T(8,128)(2,1)S(1)} %copy-done.5, bf16[2,2,208,768]{3,2,1,0:T(8,128)(2,1)} %get-tuple-element.81.r1_ref, bf16[2,768,3072]{2,1,0:T(8,128)(2,1)} %win_ref.1, bf16[2,3072,768]{2,1,0:T(8,128)(2,1)} %wout_ref.1), custom_call_target="tpu_custom_call" | custom-call | flops 16000000000 | bytes 25000000 | tf_op jit(solution)/shard_map/frozen/pallas_call | solution.py:589
  288.8 1.1 copy-done.6
  289.9 1.0 copy-done.7
  290.9 28.6 %back.2 = (bf16[512,768]{1,0:T(8,128)(2,1)}, bf16[512,768]{1,0:T(8,128)(2,1)}, bf16[512,768]{1,0:T(8,128)(2,1)}, bf16[512,768]{1,0:T(8,128)(2,1)}, bf16[512,768]...) custom-call(s32[4]{0:T(128)} %get-tuple-element.159.ends_ref, ...), custom_call_target="tpu_custom_call" | custom-call | flops 16000000000 | bytes 25000000 | tf_op jit(solution)/shard_map/back/pallas_call | solution.py:647
  319.6 29.0 %back.3 = (bf16[512,768]{1,0:T(8,128)(2,1)}, bf16[512,768]{1,0:T(8,128)(2,1)}, bf16[512,768]{1,0:T(8,128)(2,1)}, bf16[512,768]{1,0:T(8,128)(2,1)}, bf16[512,768]...) custom-call(s32[4]{0:T(128)} %get-tuple-element.160.ends_ref, ...), custom_call_target="tpu_custom_call" | custom-call | flops 16000000000 | bytes 25000000 | tf_op jit(solution)/shard_map/back/pallas_call | solution.py:647
  348.6 10.3 %weights.1 = bf16[4,768,768]{2,1,0:T(8,128)(2,1)} custom-call(bf16[512,768]{1,0:T(8,128)(2,1)S(1)} %copy-done, bf16[512,768]{1,0:T(8,128)(2,1)S(1)} %copy-done.1, bf16[512,768]{1,0:T(8,128)(2,1)S(1)} %copy-done.2, bf16[512,768]{1,0:T(8,128)(2,1)S(1)} %copy-done.3, bf16[512,768]{1,0:T(8,128)(2,1)S(1)} %copy-done.4, ...), custom_call_target="tpu_custom_call" | custom-call | tf_op jit(solution)/shard_map/weights/pallas_call | solution.py:694
  358.9 6.0 copy.37
  364.9 3.3 copy.39
  368.3 0.6 reduce-scatter.6.cloned.1.call-update
  369.2 39.3 %all-reduce.1 = f32[768,10]{0,1:T(8,128)S(1)} all-reduce(f32[768,10]{0,1:T(8,128)S(1)} %maximum_bitcast_fusion), channel_id=3, replica_groups=mesh['dp'=8,'expert'=4] {'dp','expert'}, use_global_device_ids=true, to_apply=%region_1.2.clone | all-reduce | flops 7680 | bytes 61440
  409.1 0.7 constant_dynamic-slice_fusion
  409.8 1.3 pad_maximum_fusion.1
  411.1 0.6 copy-done.13
  411.7 1.3 pad_maximum_fusion
  413.0 60.9 %reduce-scatter.8.cloned.1.call-done = bf16[24,3072]{1,0:T(8,128)(2,1)} async-done(((bf16[768,3072]{1,0:T(8,128)(2,1)}), bf16[24,3072]{1,0:T(8,128)(2,1)}) %reduce-scatter.8.cloned.1.call-update) | async-done | bytes 147472
  473.9 1.0 reshape.78
  474.9 0.7 slice_bitcast_fusion.6
  475.6 164.9 %reduce-scatter.6.cloned.1.call-done = bf16[1,2,768,384]{3,2,1,0:T(8,128)(2,1)} async-done(((bf16[8,2,768,384]{3,2,1,0:T(8,128)(2,1)}), bf16[1,2,768,384]{3,2,1,0:T(8,128)(2,1)}) %reduce-scatter.6.cloned.1.call-update) | async-done | bytes 1179664 | tf_op jit(solution)/shard_map/reduce_scatter | solution.py:642
  640.5 2.4 convert_bitcast_fusion
  643.0 1.4 copy.34
  (70 shorter events, 4.6 us)
Async XLA Ops:
  7.2 1.7 copy-start.10
  7.2 144.4 %all-gather.3.cloned.1.call-start = ((), (), s32[]{:S(2)}) async-start(), calls=%async_computation.7 | async-start | bytes 10616832 | tf_op jit(solution)/shard_map/all_gather | solution.py:537
  8.9 1.3 copy-start.19
  8.9 1.3 copy-start.20
  8.9 1.3 copy-start.21
  8.9 1.3 copy-start.22
  9.0 1.3 copy-start.17
  9.0 1.9 copy-start.24
  9.0 3.2 copy-start.23
  9.0 3.8 copy-start.18
  9.0 4.4 copy-start.9
  37.3 35.0 %all-to-all-start = ((bf16[4,2,208,768]{3,2,1,0:T(8,128)(2,1)}), bf16[4,2,208,768]{3,2,1,0:T(8,128)(2,1)S(1)}, u32[]{:S(2)}, u32[]{:S(2)}) async-start(bf16[4,2,208,768]{3,2,1,0:T(8,128)(2,1)} %get-tuple-element.83), calls=%async_computation | async-start | bytes 5111808 | tf_op jit(solution)/shard_map/all_to_all | solution.py:584
  72.4 35.1 %copy-start.8 = (bf16[4,2,208,768]{3,2,1,0:T(8,128)(2,1)}, bf16[4,2,208,768]{3,2,1,0:T(8,128)(2,1)S(1)}, u32[]{:S(2)}) copy-start(bf16[4,2,208,768]{3,2,1,0:T(8,128)(2,1)S(1)} %all-to-all-done.r0_ref) | copy-start | bytes 7667716
  254.9 4.9 copy-start.5
  254.9 64.6 %all-to-all-start.3 = ((bf16[4,2,208,768]{3,2,1,0:T(8,128)(2,1)}), bf16[4,2,208,768]{3,2,1,0:T(8,128)(2,1)}, u32[]{:S(2)}, u32[]{:S(2)}) async-start(bf16[4,2,208,768]{3,2,1,0:T(8,128)(2,1)} %get-tuple-element.98), calls=%async_computation.3 | async-start | bytes 5111808 | tf_op jit(solution)/shard_map/all_to_all | solution.py:639
  259.6 214.3 %reduce-scatter.8.cloned.1.call-start = ((), (), s32[]{:S(2)}) async-start(), calls=%async_computation.8 | async-start | bytes 4866048
  288.8 1.1 copy-start.6
  289.9 1.0 copy-start.7
  319.5 29.0 %copy-start = (bf16[512,768]{1,0:T(8,128)(2,1)S(1)}, bf16[512,768]{1,0:T(8,128)(2,1)}, u32[]{:S(2)}) copy-start(bf16[512,768]{1,0:T(8,128)(2,1)} %get-tuple-element.104.refs_0_) | copy-start | bytes 2359300
  319.5 29.0 %copy-start.1 = (bf16[512,768]{1,0:T(8,128)(2,1)S(1)}, bf16[512,768]{1,0:T(8,128)(2,1)}, u32[]{:S(2)}) copy-start(bf16[512,768]{1,0:T(8,128)(2,1)} %get-tuple-element.73.o_ref.refs_1_) | copy-start | bytes 2359300
  319.5 29.0 %copy-start.2 = (bf16[512,768]{1,0:T(8,128)(2,1)S(1)}, bf16[512,768]{1,0:T(8,128)(2,1)}, u32[]{:S(2)}) copy-start(bf16[512,768]{1,0:T(8,128)(2,1)} %get-tuple-element.105.refs_2_) | copy-start | bytes 2359300
  319.5 29.0 %copy-start.3 = (bf16[512,768]{1,0:T(8,128)(2,1)S(1)}, bf16[512,768]{1,0:T(8,128)(2,1)}, u32[]{:S(2)}) copy-start(bf16[512,768]{1,0:T(8,128)(2,1)} %get-tuple-element.106.refs_3_) | copy-start | bytes 2359300
  319.5 29.0 %copy-start.4 = (bf16[512,768]{1,0:T(8,128)(2,1)S(1)}, bf16[512,768]{1,0:T(8,128)(2,1)}, u32[]{:S(2)}) copy-start(bf16[512,768]{1,0:T(8,128)(2,1)} %get-tuple-element.107.refs_4_) | copy-start | bytes 2359300
  368.2 272.4 %reduce-scatter.6.cloned.1.call-start = ((), (), s32[]{:S(2)}) async-start(), calls=%async_computation.6 | async-start | bytes 10616832 | tf_op jit(solution)/shard_map/reduce_scatter | solution.py:642
  368.2 0.9 copy-start.15
  368.2 0.9 copy-start.16
  368.2 41.5 %copy-start.12 = (bf16[512,768]{1,0:T(8,128)(2,1)S(1)}, bf16[512,768]{1,0:T(8,128)(2,1)}, u32[]{:S(2)}) copy-start(bf16[512,768]{1,0:T(8,128)(2,1)} %get-tuple-element.100) | copy-start | bytes 2359300
  368.2 41.5 %copy-start.14 = (bf16[512,768]{1,0:T(8,128)(2,1)S(1)}, bf16[512,768]{1,0:T(8,128)(2,1)}, u32[]{:S(2)}) copy-start(bf16[512,768]{1,0:T(8,128)(2,1)} %get-tuple-element.101) | copy-start | bytes 2359300
  409.8 1.3 copy-start.11
  409.8 1.9 copy-start.13
Sparse Core Ops, SparseCore 0:
  10.8 140.7 all-gather.2
  368.3 105.5 reduce-scatter.7
  477.9 162.5 reduce-scatter.5

commit v2 on v1

--- a/solution.py
+++ b/solution.py
@@ -484,14 +484,179 @@
     def _(i):
         cols = pl.ds(pl.multiple_of(i * TILE, TILE), TILE)
         for part in range(4):
-            total = None
-            for m in range(micro):
-                a1, o, dq, dk, dv, db = ins[6 * m : 6 * m + 6]
-                left = o if part == 3 else a1
-                right = (dq, dk, dv, db)[part]
-                step = mm(left[:, cols], right[...], TN)
-                total = step if total is None else total + step
+            total = weight_grad(ins, micro, part, cols)
             dw_ref[part, cols, :] = total.astype(HALF)
+
+
+def weight_grad(ins, micro, part, cols):
+    total = None
+    for m in range(micro):
+        a1, o, dq, dk, dv, db = ins[6 * m : 6 * m + 6]
+        left = o if part == 3 else a1
+        right = (dq, dk, dv, db)[part]
+        step = mm(left[:, cols], right[...], TN)
+        total = step if total is None else total + step
+    return total
+
+
+def reduce_kernel(micro, *refs):
+    ins, smalls = refs[: 6 * micro], refs[6 * micro : 7 * micro]
+    out_ref, tiny_ref, pay, got, tiny, tiny_got, send_sem, recv_sem = refs[7 * micro :]
+    zs, xs, ys, cs, rows_all, width = pay.shape
+    rows = rows_all // 4
+    pair = 2 * rows
+    dp, ex = lax.axis_index("dp"), lax.axis_index("expert")
+    z, x, y, c = dp // xs, dp % xs, ex // cs, ex % cs
+
+    def device(zz, xx, yy, cc):
+        return (zz * xs + xx, yy * cs + cc)
+
+    others = [(z + step) % zs for step in range(1, zs)]
+    core = device(z, x, y, 1 - c)
+    side = device(z, 1 - x, y, c)
+    deep = device(z, x, 1 - y, c)
+    column = [device(zz, x, y, c) for zz in others]
+    peers = [core, side, deep] + column
+    barrier = pltpu.get_barrier_semaphore()
+    for peer in peers:
+        pl.semaphore_signal(barrier, inc=1, device_id=peer, device_id_type=pl.DeviceIdType.MESH)
+    pl.semaphore_wait(barrier, len(peers))
+
+    count = [0]
+
+    def send(source, target, peer):
+        copy = pltpu.make_async_remote_copy(
+            src_ref=source,
+            dst_ref=target,
+            send_sem=send_sem.at[count[0]],
+            recv_sem=recv_sem.at[count[0]],
+            device_id=peer,
+            device_id_type=pl.DeviceIdType.MESH,
+        )
+        count[0] += 1
+        copy.start()
+        return copy
+
+    def produce(parts, base):
+        tile = 16 * rows
+        for j in range(width // tile):
+            cols = slice(j * tile, (j + 1) * tile)
+            for at, part in enumerate(parts):
+                total = weight_grad(ins, micro, part, cols).astype(HALF)
+                for i in range(16):
+                    number = 16 * j + i
+                    place = (
+                        number // (ys * cs) // xs,
+                        number // (ys * cs) % xs,
+                        number % (ys * cs) // cs,
+                        number % cs,
+                    )
+                    pay[place + (slice(base + at * rows, base + (at + 1) * rows),)] = total[
+                        i * rows : (i + 1) * rows, :
+                    ]
+
+    def add(place, band, held):
+        pay[place + (band,)] = (
+            pay[place + (band,)].astype(SINGLE) + held[...].astype(SINGLE)
+        ).astype(HALF)
+
+    top, low = pl.ds(0, pair), pl.ds(pair, pair)
+    core_a, core_b, deep_a, side_b, side_a, col_b, col_a, deep_b = got
+    total = smalls[0][...]
+    for ref in smalls[1:]:
+        total = total + ref[...]
+    tiny[...] = total
+
+    produce((3, 2), 0)
+    first = send(pay.at[:, :, :, 1 - c, top], core_a, core)
+    tiny_core = send(tiny, tiny_got.at[0], core)
+    produce((0, 1), pair)
+    second = send(pay.at[:, :, :, 1 - c, low], core_b, core)
+
+    first.wait()
+
+    @pl.loop(0, zs)
+    def _(i):
+        for xx in range(xs):
+            for yy in range(ys):
+                add((i, xx, yy, c), top, core_a.at[i, xx, yy])
+
+    third = send(pay.at[:, :, 1 - y, c, top], deep_a, deep)
+    tiny_core.wait()
+    tiny[...] += tiny_got[0]
+    tiny_deep = send(tiny, tiny_got.at[1], deep)
+    second.wait()
+
+    @pl.loop(0, zs)
+    def _(i):
+        for xx in range(xs):
+            for yy in range(ys):
+                add((i, xx, yy, c), low, core_b.at[i, xx, yy])
+
+    fourth = send(pay.at[:, 1 - x, :, c, low], side_b, side)
+    tiny_deep.wait()
+    tiny[...] += tiny_got[1]
+    tiny_side = send(tiny, tiny_got.at[2], side)
+
+    third.wait()
+
+    @pl.loop(0, zs)
+    def _(i):
+        for xx in range(xs):
+            add((i, xx, y, c), top, deep_a.at[i, xx])
+
+    fifth = send(pay.at[:, 1 - x, y, c, top], side_a, side)
+    tiny_side.wait()
+    tiny[...] += tiny_got[2]
+    tiny_col = [send(tiny, tiny_got.at[3 + i], peer) for i, peer in enumerate(column)]
+
+    fourth.wait()
+
+    @pl.loop(0, zs)
+    def _(i):
+        for yy in range(ys):
+            add((i, x, yy, c), low, side_b.at[i, yy])
+
+    sixth = [
+        send(pay.at[zz, x, :, c, low], col_b.at[i], peer)
+        for i, (zz, peer) in enumerate(zip(others, column))
+    ]
+    fifth.wait()
+
+    @pl.loop(0, zs)
+    def _(i):
+        add((i, x, y, c), top, side_a.at[i])
+
+    seventh = [
+        send(pay.at[zz, x, y, c, top], col_a.at[i], peer)
+        for i, (zz, peer) in enumerate(zip(others, column))
+    ]
+    for copy in sixth:
+        copy.wait()
+    for yy in range(ys):
+        place = (z, x, yy, c, low)
+        total = pay[place].astype(SINGLE)
+        for i in range(zs - 1):
+            total = total + col_b[i, yy].astype(SINGLE)
+        pay[place] = total.astype(HALF)
+    eighth = send(pay.at[z, x, 1 - y, c, low], deep_b, deep)
+    for copy in seventh:
+        copy.wait()
+    total = pay[z, x, y, c, 0:pair].astype(SINGLE)
+    for i in range(zs - 1):
+        total = total + col_a[i].astype(SINGLE)
+    out_ref[3] = total[0:rows]
+    out_ref[2] = total[rows:pair]
+    for copy in tiny_col:
+        copy.wait()
+    total = tiny[...]
+    for i in range(zs - 1):
+        total = total + tiny_got[3 + i]
+    tiny_ref[...] = total
+    eighth.wait()
+    total = pay[z, x, y, c, pair : 2 * pair].astype(SINGLE) + deep_b[...].astype(SINGLE)
+    out_ref[0] = total[0:rows]
+    out_ref[1] = total[rows:pair]
 
 
 def vmem(count):
@@ -691,19 +856,55 @@
         small_list.append(small)
         weight_ins += [a1, o, dq, dk, dv, db]
 
-    grads = pl.pallas_call(
-        weights_kernel,
-        out_shape=shape((4, width, width), HALF),
-        in_specs=vmem(len(weight_ins)),
-        out_specs=vmem(1)[0],
-        compiler_params=params(50),
-        name="weights",
-    )(*weight_ins)
-    shared = lax.psum_scatter(grads, ("dp", "expert"), scatter_dimension=1, tiled=True)
-    small = sum(small_list[1:], small_list[0])
-    small = jnp.concatenate([small[:experts], small[rows16 : rows16 + 4]], 0).T
-    small = lax.psum_scatter(small, ("dp", "expert"), scatter_dimension=0, tiled=True)
-    shared = shared.astype(SINGLE)
+    pieces = dp * owners
+    if dp == 8 and owners == 4:
+        zs, xs, ys, cs = 4, 2, 2, 2
+        rows = width // pieces
+        pair = 2 * rows
+        landing = [
+            (zs, xs, ys),
+            (zs, xs, ys),
+            (zs, xs),
+            (zs, ys),
+            (zs,),
+            (zs - 1, ys),
+            (zs - 1,),
+            (),
+        ]
+        small_rows = small_list[0].shape[0]
+        shared, small = pl.pallas_call(
+            functools.partial(reduce_kernel, micro),
+            out_shape=[shape((4, rows, width), SINGLE), shape((small_rows, width), SINGLE)],
+            in_specs=vmem(7 * micro),
+            out_specs=vmem(2),
+            scratch_shapes=[
+                pltpu.VMEM((zs, xs, ys, cs, 4 * rows, width), HALF),
+                [pltpu.VMEM(lead + (pair, width), HALF) for lead in landing],
+                pltpu.VMEM((small_rows, width), SINGLE),
+                pltpu.VMEM((zs + 2, small_rows, width), SINGLE),
+                pltpu.SemaphoreType.DMA((18,)),
+                pltpu.SemaphoreType.DMA((18,)),
+            ],
+            compiler_params=params(56, collective_id=1, has_side_effects=True),
+            name="reduce",
+        )(*weight_ins, *small_list)
+        small = jnp.concatenate([small[:experts], small[rows16 : rows16 + 4]], 0)
+        at = (lax.axis_index("dp") * owners + lax.axis_index("expert")) * rows
+        small = lax.dynamic_slice_in_dim(small, at, rows, 1).T
+    else:
+        grads = pl.pallas_call(
+            weights_kernel,
+            out_shape=shape((4, width, width), HALF),
+            in_specs=vmem(len(weight_ins)),
+            out_specs=vmem(1)[0],
+            compiler_params=params(50),
+            name="weights",
+        )(*weight_ins)
+        shared = lax.psum_scatter(grads, ("dp", "expert"), scatter_dimension=1, tiled=True)
+        shared = shared.astype(SINGLE)
+        small = sum(small_list[1:], small_list[0])
+        small = jnp.concatenate([small[:experts], small[rows16 : rows16 + 4]], 0).T
+        small = lax.psum_scatter(small, ("dp", "expert"), scatter_dimension=0, tiled=True)
     return (
         jnp.stack(mixed_list, 0),
         jnp.stack(xgrad_list, 0),

time: 657 us -> 431 us (0.66)
  waiting for transfers between devices: 280 us -> 53.8 us
  Pallas kernels: 207 us -> 255 us
  blocking collectives: 110 us -> 69 us
  local copies, waits for them, and re-layouts: 23.8 us -> 16.3 us
    reduce_scatter x1, waiting for transfers between devices: 165 us -> 0.01 us  [per_device(): lax.psum_scatter(grads_w, 'dp', scatter_dimension=0, tiled=True)[0]]
    unnamed x4 -> x2, waiting for transfers between devices: 61.6 us -> 0.03 us
    pallas_call x1, Pallas kernels: 10.3 us -> 58.6 us  [per_device(): pl.pallas_call(functools.partial(reduce_kernel, micro), out_shape=[shape(...]
    unnamed x1 -> x0, blocking collectives: 39.3 us -> none
    unnamed x55 -> x42, local copies, waits for them, and re-layouts: 16.3 us -> 7.54 us
  transfers between devices with their start and end apart: 5 -> 4, of which waited for: 4 -> 2; matrix products, arithmetic and copies ran while one was open for 2% -> 3% of each run, Pallas kernels for 15% -> 44%
where the time goes in v2:
time: 431 us; the launch traced here: 425 us
  Pallas kernels  255 us (59%)
  blocking collectives  69 us (16%)
  waiting for transfers between devices  53.8 us (12%)
  local copies, waits for them, and re-layouts  16.3 us (4%)
  between operations  14.8 us (3%)
  starting transfers between devices  9.33 us (2%)
  other arithmetic  7.01 us (2%)
    pallas_call x1, Pallas kernels, per_device(): pl.pallas_call(owned_kernel, grid=(dp // group,), out_shape=[shape((owner...  68.2 us
    pallas_call x1, Pallas kernels, per_device(): pl.pallas_call(functools.partial(reduce_kernel, micro), out_shape=[shape(...  58.6 us
    pallas_call x2, Pallas kernels, per_device(): pl.pallas_call(functools.partial(back_kernel, capacity, experts), out_sha...  57.5 us
    all_gather x1, waiting for transfers between devices, per_device(): all_w = lax.all_gather(local_w, 'dp', axis=0, tiled=False)  44.2 us
    pallas_call x2, Pallas kernels, per_device(): pl.pallas_call(functools.partial(attend_kernel, capacity, experts, frozen...  41.7 us
    all_to_all x1, blocking collectives, per_device(): lax.all_to_all(outs[12], 'expert', split_axis=0, concat_axis=0, tiled=True)  35.1 us
    all_to_all x1, blocking collectives, per_device(): lax.all_to_all(one, 'expert', split_axis=0, concat_axis=0, tiled=True)  33.9 us
    pallas_call x1, Pallas kernels, per_device(): pl.pallas_call(frozen_kernel, grid=(frozen, ff // block), out_shape=[shap...  29 us
  transfers between devices with their start and end apart: 4, of which 2 were waited for; matrix products, arithmetic and copies ran while one was open for 3% of the time, Pallas kernels for 44%

profile of v2, /device:TPU:0, one launch (start us, length us, event | category | flops | bytes accessed | tf_op | source)
XLA Modules:
  0.0 425.3 jit_solution(17985733173460973063)
XLA Ops:
  7.2 1.6 copy.33
  9.0 1.1 pad_maximum_fusion.2
  10.3 0.6 scatter.4.wr_ref
  11.1 0.6 pad_maximum_fusion.3.norms_ref
  12.2 0.6 fusion.3
  12.8 0.6 slice_bitcast_fusion.11
  13.4 3.1 slice_bitcast_fusion.2
  16.5 20.9 %attend.2 = (bf16[512,768]{1,0:T(8,128)(2,1)}, bf16[512,768]{1,0:T(8,128)(2,1)}, bf16[512,768]{1,0:T(8,128)(2,1)}, bf16[512,768]{1,0:T(8,128)(2,1)}, bf16[512,76...) custom-call(s32[4]{0:T(128)} %get-tuple-element.163.ends_ref, ...), custom_call_target="tpu_custom_call" | custom-call | flops 8000000000 | bytes 20000000 | tf_op jit(solution)/shard_map/attend/pallas_call | solution.py:712
  37.3 4.2 all-to-all-start
  41.8 20.9 %attend.3 = (bf16[512,768]{1,0:T(8,128)(2,1)}, bf16[512,768]{1,0:T(8,128)(2,1)}, bf16[512,768]{1,0:T(8,128)(2,1)}, bf16[512,768]{1,0:T(8,128)(2,1)}, bf16[512,76...) custom-call(s32[4]{0:T(128)} %get-tuple-element.164.ends_ref, ...), custom_call_target="tpu_custom_call" | custom-call | flops 8000000000 | bytes 20000000 | tf_op jit(solution)/shard_map/attend/pallas_call | solution.py:712
  62.7 9.6 %all-to-all-done.r0_ref = bf16[4,2,208,768]{3,2,1,0:T(8,128)(2,1)S(1)} async-done(((bf16[4,2,208,768]{3,2,1,0:T(8,128)(2,1)}), bf16[4,2,208,768]{3,2,1,0:T(8,128)(2,1)S(1)}, u32[]{:S(2)}, u32[]{:S(2)}) %all-to-all-start) | async-done | bytes 2555936 | tf_op jit(solution)/shard_map/all_to_all | solution.py:749
  72.2 35.1 %all_to_all.20.r1_ref = bf16[4,2,208,768]{3,2,1,0:T(8,128)(2,1)} all-to-all(bf16[4,2,208,768]{3,2,1,0:T(8,128)(2,1)} %get-tuple-element.86), channel_id=1, replica_groups=mesh['dp'=8,'expert'=4] {'expert'}, dimensions={0} | all-to-all | bytes 5111808 | tf_op jit(solution)/shard_map/all_to_all | solution.py:749
  107.4 44.2 %all-gather.3.cloned.1.call-done = bf16[16,384,768]{2,1,0:T(8,128)(2,1)} async-done(((bf16[2,384,768]{2,1,0:T(8,128)(2,1)}), bf16[16,384,768]{2,1,0:T(8,128)(2,1)}) %all-gather.3.cloned.1.call-update) | async-done | bytes 9437200 | tf_op jit(solution)/shard_map/all_gather | solution.py:702
  151.6 68.2 %owned.1 = (bf16[4,2,208,768]{3,2,1,0:T(8,128)(2,1)}, bf16[4,2,208,768]{3,2,1,0:T(8,128)(2,1)}, bf16[8,2,768,384]{3,2,1,0:T(8,128)(2,1)}) custom-call(bf16[4,2,208,768]{3,2,1,0:T(8,128)(2,1)} %copy-done.3, bf16[4,2,208,768]{3,2,1,0:T(8,128)(2,1)} %all_to_all.20.r1_ref, bf16[8,2,384,768]{3,2,1,0:T(8,128)(2,1)} %bitcast.71), custom_call_target="tpu_custom_call" | custom-call | flops 46999998464 | bytes 35000000 | tf_op jit(solution)/shard_map/owned/pallas_call | solution.py:780
  219.8 1.7 copy-done.4
  221.5 33.9 %all_to_all.21.back_ref = bf16[4,2,208,768]{3,2,1,0:T(8,128)(2,1)} all-to-all(bf16[4,2,208,768]{3,2,1,0:T(8,128)(2,1)S(1)} %copy-done.4), channel_id=1, replica_groups=mesh['dp'=8,'expert'=4] {'expert'}, dimensions={0} | all-to-all | bytes 5111808 | tf_op jit(solution)/shard_map/all_to_all | solution.py:804
  255.4 4.9 %all-to-all-start.3 = ((bf16[4,2,208,768]{3,2,1,0:T(8,128)(2,1)}), bf16[4,2,208,768]{3,2,1,0:T(8,128)(2,1)}, u32[]{:S(2)}, u32[]{:S(2)}) async-start(bf16[4,2,208,768]{3,2,1,0:T(8,128)(2,1)} %get-tuple-element.100), calls=%async_computation.3 | async-start | bytes 5111808 | tf_op jit(solution)/shard_map/all_to_all | solution.py:804
  260.3 29.0 %frozen.1 = (bf16[2,2,208,768]{3,2,1,0:T(8,128)(2,1)S(1)}, bf16[2,2,208,768]{3,2,1,0:T(8,128)(2,1)S(1)}) custom-call(bf16[2,2,208,768]{3,2,1,0:T(8,128)(2,1)S(1)} %copy-done, bf16[2,2,208,768]{3,2,1,0:T(8,128)(2,1)} %get-tuple-element.83.r1_ref, bf16[2,768,3072]{2,1,0:T(8,128)(2,1)} %win_ref.1, bf16[2,3072,768]{2,1,0:T(8,128)(2,1)} %wout_ref.1), custom_call_target="tpu_custom_call" | custom-call | flops 16000000000 | bytes 25000000 | tf_op jit(solution)/shard_map/frozen/pallas_call | solution.py:754
  289.3 1.1 copy-done.1
  290.4 1.0 copy-done.2
  291.4 28.7 %back.2 = (bf16[512,768]{1,0:T(8,128)(2,1)}, bf16[512,768]{1,0:T(8,128)(2,1)}, bf16[512,768]{1,0:T(8,128)(2,1)}, bf16[512,768]{1,0:T(8,128)(2,1)}, bf16[512,768]...) custom-call(s32[4]{0:T(128)} %get-tuple-element.163.ends_ref, ...), custom_call_target="tpu_custom_call" | custom-call | flops 16000000000 | bytes 25000000 | tf_op jit(solution)/shard_map/back/pallas_call | solution.py:812
  320.1 28.9 %back.3 = (bf16[512,768]{1,0:T(8,128)(2,1)}, bf16[512,768]{1,0:T(8,128)(2,1)}, bf16[512,768]{1,0:T(8,128)(2,1)}, bf16[512,768]{1,0:T(8,128)(2,1)}, bf16[512,768]...) custom-call(s32[4]{0:T(128)} %get-tuple-element.164.ends_ref, ...), custom_call_target="tpu_custom_call" | custom-call | flops 16000000000 | bytes 25000000 | tf_op jit(solution)/shard_map/back/pallas_call | solution.py:812
  349.0 58.6 %reduce.3 = (f32[4,24,768]{2,1,0:T(8,128)}, f32[24,768]{1,0:T(8,128)}) custom-call(bf16[512,768]{1,0:T(8,128)(2,1)} %get-tuple-element.104.refs_0_, bf16[512,768]{1,0:T(8,128)(2,1)} %get-tuple-element.75.o_ref.refs_1_, bf16[512,768]{1,0:T(8,128)(2,1)} %get-tuple-element.105.refs_2_, bf16[512,768]{1,0:T(8,128)(2,1)} %get-tuple-element.106.refs_3_, ...), custom_call_target="tpu_custom_call" | custom-call | tf_op jit(solution)/shard_map/reduce/pallas_call | solution.py:875
  407.6 0.7 slice.105
  408.3 0.7 slice.106
  409.1 0.6 slice.124
  409.7 1.3 pad_maximum_fusion.1
  411.1 0.6 copy-done.9
  411.7 1.3 pad_maximum_fusion
  413.5 0.7 slice_bitcast_fusion.6
  414.2 2.4 convert_bitcast_fusion
  416.6 1.4 copy.34
  (51 shorter events, 1.7 us)
Async XLA Ops:
  7.2 1.7 copy-start.6
  7.2 144.4 %all-gather.3.cloned.1.call-start = ((), (), s32[]{:S(2)}) async-start(), calls=%async_computation.6 | async-start | bytes 10616832 | tf_op jit(solution)/shard_map/all_gather | solution.py:702
  8.9 1.3 copy-start.14
  8.9 1.3 copy-start.15
  8.9 1.3 copy-start.16
  8.9 1.3 copy-start.17
  9.0 1.3 copy-start.12
  9.0 1.9 copy-start.19
  9.0 3.2 copy-start.18
  9.0 3.8 copy-start.13
  9.0 4.4 %copy-start.5 = (bf16[2,512,768]{2,1,0:T(8,128)(2,1)S(1)}, bf16[2,512,768]{2,1,0:T(8,128)(2,1)}, u32[]{:S(2)}) copy-start(bf16[2,512,768]{2,1,0:T(8,128)(2,1)} %param.37) | copy-start | bytes 4718596
  37.3 34.9 %all-to-all-start = ((bf16[4,2,208,768]{3,2,1,0:T(8,128)(2,1)}), bf16[4,2,208,768]{3,2,1,0:T(8,128)(2,1)S(1)}, u32[]{:S(2)}, u32[]{:S(2)}) async-start(bf16[4,2,208,768]{3,2,1,0:T(8,128)(2,1)} %get-tuple-element.85), calls=%async_computation | async-start | bytes 5111808 | tf_op jit(solution)/shard_map/all_to_all | solution.py:749
  41.6 372.6 %reduce-scatter.2.cloned.1.call-start = ((), (), s32[]{:S(2)}) async-start(), calls=%async_computation.5 | async-start | bytes 10616832 | tf_op jit(solution)/shard_map/reduce_scatter | solution.py:807
  72.2 35.2 %copy-start.3 = (bf16[4,2,208,768]{3,2,1,0:T(8,128)(2,1)}, bf16[4,2,208,768]{3,2,1,0:T(8,128)(2,1)S(1)}, u32[]{:S(2)}) copy-start(bf16[4,2,208,768]{3,2,1,0:T(8,128)(2,1)S(1)} %all-to-all-done.r0_ref) | copy-start | bytes 7667716
  219.8 1.7 copy-start.4
  255.4 4.9 %copy-start = (bf16[2,2,208,768]{3,2,1,0:T(8,128)(2,1)S(1)}, bf16[2,2,208,768]{3,2,1,0:T(8,128)(2,1)}, u32[]{:S(2)}) copy-start(bf16[2,2,208,768]{3,2,1,0:T(8,128)(2,1)} %get-tuple-element.82.r0_ref) | copy-start | bytes 3833860
  255.4 64.7 %all-to-all-start.3 = ((bf16[4,2,208,768]{3,2,1,0:T(8,128)(2,1)}), bf16[4,2,208,768]{3,2,1,0:T(8,128)(2,1)}, u32[]{:S(2)}, u32[]{:S(2)}) async-start(bf16[4,2,208,768]{3,2,1,0:T(8,128)(2,1)} %get-tuple-element.100), calls=%async_computation.3 | async-start | bytes 5111808 | tf_op jit(solution)/shard_map/all_to_all | solution.py:804
  289.3 1.1 copy-start.1
  290.4 1.1 copy-start.2
  349.0 60.8 %copy-start.8 = (bf16[512,768]{1,0:T(8,128)(2,1)S(1)}, bf16[512,768]{1,0:T(8,128)(2,1)}, u32[]{:S(2)}) copy-start(bf16[512,768]{1,0:T(8,128)(2,1)} %get-tuple-element.102) | copy-start | bytes 2359300
  349.0 60.8 %copy-start.10 = (bf16[512,768]{1,0:T(8,128)(2,1)S(1)}, bf16[512,768]{1,0:T(8,128)(2,1)}, u32[]{:S(2)}) copy-start(bf16[512,768]{1,0:T(8,128)(2,1)} %get-tuple-element.103) | copy-start | bytes 2359300
  409.7 1.3 copy-start.7
  409.7 1.9 copy-start.9
  411.7 1.8 copy-start.11
Sparse Core Ops, SparseCore 0:
  10.8 140.7 all-gather.2
  219.9 161.6 reduce-scatter.1
